TPU v7x, 256 devices: a whole 4x4x8 slice. The times are simulated.
256 devices in a mesh: dp: 8 (over x, core), ctx: 32 (over z, y).
Axes of the slice: x: 4, y: 4, z: 8, core: 2. Of those that a mesh axis runs over, the one named last changes fastest.
Arguments:
- pre_q: bfloat16 [16384, 4096], P(('dp', 'ctx')), may hold values from -6 to 6
- prefix_keys: bfloat16 [16384, 512], P(('dp', 'ctx')), may hold values from -6 to 6
- prefix_values: bfloat16 [16384, 512], P(('dp', 'ctx')), may hold values from -6 to 6
- pre_cot: bfloat16 [16384, 4096], P(('dp', 'ctx')), may hold values from -6 to 6
- gen_q: bfloat16 [16384, 4096], P(('dp', 'ctx')), may hold values from -6 to 6
- rollout_keys: bfloat16 [16384, 512], P(('dp', 'ctx')), may hold values from -6 to 6
- rollout_values: bfloat16 [16384, 512], P(('dp', 'ctx')), may hold values from -6 to 6
- gen_cot: bfloat16 [16384, 4096], P(('dp', 'ctx')), may hold values from -6 to 6
- q_gain: float32 [128], replicated, may hold values from 0.5 to 1.5
- k_gain: float32 [128], replicated, may hold values from 0.5 to 1.5
- piece_dest: int32 [8, 256], P('dp'), may hold values from 0 to 255, as said below
- prefix_parent: int32 [8, 32], P('dp'), may hold values from -1 to 31, as said below
- branch_parent: int32 [8, 32], P('dp'), may hold values from 0 to 31
- rewards: int32 [8, 32], P('dp'), may hold values from 0 to 9
Outputs:
- query_gradient: bfloat16 [32768, 4096], P(('dp', 'ctx'))
- key_gradient: bfloat16 [32768, 512], P(('dp', 'ctx'))
- grad_v: bfloat16 [32768, 512], P(('dp', 'ctx'))
- q_gain_grad: float32 [128], replicated
- k_gain_grad: float32 [128], replicated
Inputs may be any that keep to these rules, and one draw needn't show every extreme that they name: `piece_dest`: each row (one group) is a permutation; the pieces of one device go to any one device at most 1 times, and exactly 1 times for some pair. `prefix_parent`: in each row, half of the prefix nodes (rounded down) are roots with -1; every other one names a root of the same row.
All inputs are finite; a program needn't handle non-finite values.
Results may differ from a plain program's by a relative error of at most 0.013.
Values may be sent and summed in bfloat16 or wider, within the bound.
A program may use at most 128 MiB of HBM per device.

v0:
```python
import math

import jax
import jax.numpy as jnp
from jax import lax
from jax.sharding import PartitionSpec as P

PIECES = 8


EPSILON = 1e-06


def norm_heads(values, gain):
    inverse = lax.rsqrt(jnp.mean(values * values, axis=-1, keepdims=True) + EPSILON)
    return (values * inverse * gain, inverse)


def norm_back(values, inverse, gain, upstream):
    scaled = gain * upstream
    inner = jnp.mean(values * scaled, axis=-1, keepdims=True)
    result = inverse * scaled - values * (inverse * inverse * inverse) * inner
    gain_term = jnp.sum((upstream * values * inverse).reshape(-1, values.shape[-1]), axis=0)
    return (result, gain_term)


def advantages(rewards_row, prefix_row, branch_row):
    row_count = prefix_row.shape[0]
    match_prefix = branch_row[:, None] == jnp.arange(row_count, dtype=jnp.int32)[None, :]
    upper = jnp.sum(jnp.where(match_prefix, prefix_row[None, :], 0), axis=1)
    rooted = jnp.where(upper >= 0, upper, branch_row)
    member = (rooted[:, None] == rooted[None, :]).astype(jnp.float32)
    score = rewards_row.astype(jnp.float32)
    sizes = jnp.sum(member, axis=1)
    center = jnp.sum(member * score[None, :], axis=1) / sizes
    spread = jnp.sum(member * (score[None, :] - center[:, None]) ** 2, axis=1) / sizes
    return ((score - center) / jnp.maximum(jnp.sqrt(spread), 1.0), upper)


def node_mask(anc_ok, node):
    position = jnp.arange(node, dtype=jnp.int32)
    own = (position[None, :] <= position[:, None]).astype(jnp.float32)
    tree_nodes = anc_ok.shape[0]
    own = jnp.broadcast_to(own, (tree_nodes, node, node))
    far = jnp.broadcast_to(
        jnp.repeat(anc_ok, node, axis=1)[:, None, :], (tree_nodes, node, 2 * node)
    )
    return jnp.concatenate([own, far], axis=2)[:, None, None]


def masked_weights(query_bfloat, keys_bf, anc_ok):
    scale = 1.0 / math.sqrt(query_bfloat.shape[-1])
    scores = (
        jnp.einsum("nqcgd,nkcd->ncgqk", query_bfloat, keys_bf, preferred_element_type=jnp.float32)
        * scale
    )
    return jnp.exp(scores) * node_mask(anc_ok, query_bfloat.shape[1])


def attend_grads(query_bfloat, keys_bf, vals_bf, cotangent_bfloat, anc_ok, totals):
    scale = 1.0 / math.sqrt(query_bfloat.shape[-1])
    weights = masked_weights(query_bfloat, keys_bf, anc_ok)
    totals = jnp.sum(weights, axis=-1, keepdims=True)
    probs = weights / totals
    probs_bf = probs.astype(jnp.bfloat16)
    dprob = jnp.einsum(
        "nqcgd,nkcd->ncgqk", cotangent_bfloat, vals_bf, preferred_element_type=jnp.float32
    )
    inner = jnp.sum(probs * dprob, axis=-1, keepdims=True)
    dscore_bf = (probs * (dprob - inner) * scale).astype(jnp.bfloat16)
    grad_query = jnp.einsum(
        "ncgqk,nkcd->nqcgd", dscore_bf, keys_bf, preferred_element_type=jnp.float32
    )
    keys_gradient_total = jnp.einsum(
        "ncgqk,nqcgd->nkcd", dscore_bf, query_bfloat, preferred_element_type=jnp.float32
    )
    values_gradient = jnp.einsum(
        "ncgqk,nqcgd->nkcd", probs_bf, cotangent_bfloat, preferred_element_type=jnp.float32
    )
    return (grad_query, keys_gradient_total, values_gradient)


def body(
    pre_q,
    prefix_keys,
    prefix_values,
    pre_cot,
    gen_q,
    rollout_keys,
    rollout_values,
    gen_cot,
    q_gain,
    k_gain,
    piece_dest,
    prefix_parent,
    branch_parent,
    rewards,
):
    row_count = lax.axis_size("ctx")
    device = lax.axis_index("ctx")
    node = pre_q.shape[0]
    branches = gen_q.shape[0] // node
    tree_nodes = 1 + branches
    head_dim = q_gain.shape[0]
    heads = pre_q.shape[1] // head_dim
    kv_heads = prefix_keys.shape[1] // head_dim
    heads_per_group = heads // kv_heads
    pieces = PIECES
    seg_rows = gen_q.shape[0] // pieces
    most = max(1, 2 * pieces // row_count)
    table = piece_dest[0].reshape(row_count, pieces)
    mine = lax.dynamic_index_in_dim(table, device, 0, keepdims=False)
    owner = mine // pieces
    order = jnp.arange(pieces, dtype=jnp.int32)
    earlier = (owner[:, None] == owner[None, :]) & (order[None, :] < order[:, None])
    send_slot = owner * most + jnp.sum(earlier, axis=1)

    def pack(row_indices):
        width = row_indices.shape[1]
        parts = row_indices.reshape(pieces, seg_rows, width)
        placed = (
            jnp.zeros((row_count * most, seg_rows, width), row_indices.dtype)
            .at[send_slot]
            .set(parts)
        )
        return placed

    moved = (
        lax.all_to_all(pack(gen_q), "ctx", split_axis=0, concat_axis=0, tiled=True),
        lax.all_to_all(pack(rollout_keys), "ctx", split_axis=0, concat_axis=0, tiled=True),
        lax.all_to_all(pack(rollout_values), "ctx", split_axis=0, concat_axis=0, tiled=True),
        lax.all_to_all(pack(gen_cot), "ctx", split_axis=0, concat_axis=0, tiled=True),
    )
    inverse = (
        jnp.zeros((row_count * pieces,), jnp.int32)
        .at[table.reshape(-1)]
        .set(jnp.arange(row_count * pieces, dtype=jnp.int32))
    )
    wanted = lax.dynamic_slice_in_dim(inverse, device * pieces, pieces)
    source = wanted // pieces
    within = wanted % pieces
    source_owner = jnp.take(table, source, axis=0) // pieces
    before = (source_owner == device) & (order[None, :] < within[:, None])
    position = source * most + jnp.sum(before, axis=1)

    def unpack(block):
        width = block.shape[2]
        return block[position].reshape(branches, node, width)

    def prefix_tree(prefix_rows, block):
        return jnp.concatenate([prefix_rows[None], unpack(block)], axis=0)

    q_tree = (
        prefix_tree(pre_q, moved[0]).astype(jnp.float32).reshape(tree_nodes, node, heads, head_dim)
    )
    key_tree_order = (
        prefix_tree(prefix_keys, moved[1])
        .astype(jnp.float32)
        .reshape(tree_nodes, node, kv_heads, head_dim)
    )
    value_tree_order = prefix_tree(prefix_values, moved[2]).reshape(
        tree_nodes, node, kv_heads, head_dim
    )
    cotangent_tree = prefix_tree(pre_cot, moved[3]).astype(jnp.float32)
    query_norm, q_inv = norm_heads(q_tree, q_gain)
    k_norm, k_inv = norm_heads(key_tree_order, k_gain)
    query_bfloat = query_norm.astype(jnp.bfloat16).reshape(
        tree_nodes, node, kv_heads, heads_per_group, head_dim
    )
    key_bf = k_norm.astype(jnp.bfloat16)
    prefix_row = prefix_parent[0]
    branch_row = branch_parent[0]
    adv, upper = advantages(rewards[0], prefix_row, branch_row)
    my_adv = lax.dynamic_slice_in_dim(adv, device * branches, branches)
    my_parent = lax.dynamic_slice_in_dim(branch_row, device * branches, branches)
    my_upper = lax.dynamic_slice_in_dim(upper, device * branches, branches)
    own_parent = lax.dynamic_index_in_dim(prefix_row, device, 0, keepdims=False)
    first_ids = jnp.stack([own_parent, jnp.full((), -1, jnp.int32)])[None]
    anc_ids = jnp.concatenate([first_ids, jnp.stack([my_parent, my_upper], axis=1)], axis=0)
    clipped_ratio = jnp.maximum(anc_ids, 0)
    valid = (anc_ids >= 0).astype(jnp.float32)
    attention_weight = jnp.concatenate([jnp.ones((1,), jnp.float32), my_adv])
    cotangent_bfloat = (
        (attention_weight[:, None, None] * cotangent_tree)
        .astype(jnp.bfloat16)
        .reshape(tree_nodes, node, kv_heads, heads_per_group, head_dim)
    )
    pre_key = key_bf[0].reshape(node, kv_heads * head_dim)
    gathered = (
        lax.all_gather(pre_key, "ctx", axis=0, tiled=True),
        lax.all_gather(prefix_values, "ctx", axis=0, tiled=True),
    )
    distant_keys = (
        gathered[0]
        .reshape(row_count, node, kv_heads, head_dim)[clipped_ratio]
        .reshape(tree_nodes, 2 * node, kv_heads, head_dim)
    )
    distant_values = (
        gathered[1]
        .reshape(row_count, node, kv_heads, head_dim)[clipped_ratio]
        .reshape(tree_nodes, 2 * node, kv_heads, head_dim)
    )
    keys_all = jnp.concatenate([key_bf, distant_keys], axis=1)
    vals_all = jnp.concatenate([value_tree_order, distant_values], axis=1)
    grads = attend_grads(query_bfloat, keys_all, vals_all, cotangent_bfloat, valid, None)
    grad_qn, keys_gradient_total, values_gradient = grads
    selector = valid[:, :, None, None, None]
    width = kv_heads * head_dim
    partial_keys = (
        keys_gradient_total[:, node:].reshape(tree_nodes, 2, node, kv_heads, head_dim) * selector
    ).reshape(tree_nodes * 2, node, width)
    partial_values = (
        values_gradient[:, node:].reshape(tree_nodes, 2, node, kv_heads, head_dim) * selector
    ).reshape(tree_nodes * 2, node, width)
    term_key_rows = (
        jnp.zeros((row_count, node, width), jnp.float32)
        .at[clipped_ratio.reshape(-1)]
        .add(partial_keys)
    )
    term_value_rows = (
        jnp.zeros((row_count, node, width), jnp.float32)
        .at[clipped_ratio.reshape(-1)]
        .add(partial_values)
    )
    summed_k, summed_v = (
        lax.psum_scatter(
            term_key_rows.reshape(row_count * node, width).astype(jnp.bfloat16),
            "ctx",
            scatter_dimension=0,
            tiled=True,
        ).astype(jnp.float32),
        lax.psum_scatter(
            term_value_rows.reshape(row_count * node, width).astype(jnp.bfloat16),
            "ctx",
            scatter_dimension=0,
            tiled=True,
        ).astype(jnp.float32),
    )
    grad_kn = keys_gradient_total[:, :node].at[0].add(summed_k.reshape(node, kv_heads, head_dim))
    value_normed_gradient = (
        values_gradient[:, :node].at[0].add(summed_v.reshape(node, kv_heads, head_dim))
    )
    query_gradient, query_norm_term = norm_back(
        q_tree, q_inv, q_gain, grad_qn.reshape(tree_nodes, node, heads, head_dim)
    )
    key_gradient, key_norm_term = norm_back(key_tree_order, k_inv, k_gain, grad_kn)
    q_sum, k_sum = lax.psum((query_norm_term, key_norm_term), ("dp", "ctx"))
    row_indices = tree_nodes * node
    return (
        query_gradient.reshape(row_indices, heads * head_dim).astype(jnp.bfloat16),
        key_gradient.reshape(row_indices, width).astype(jnp.bfloat16),
        value_normed_gradient.reshape(row_indices, width).astype(jnp.bfloat16),
        q_sum,
        k_sum,
    )


def solution(mesh):
    placed = (
        P(("dp", "ctx"), None),
        P(("dp", "ctx"), None),
        P(("dp", "ctx"), None),
        P(("dp", "ctx"), None),
        P(("dp", "ctx"), None),
        P(("dp", "ctx"), None),
        P(("dp", "ctx"), None),
        P(("dp", "ctx"), None),
        P(),
        P(),
        P("dp", None),
        P("dp", None),
        P("dp", None),
        P("dp", None),
    )
    return jax.shard_map(
        body,
        mesh=mesh,
        in_specs=placed,
        out_specs=(
            P(("dp", "ctx"), None),
            P(("dp", "ctx"), None),
            P(("dp", "ctx"), None),
            P(),
            P(),
        ),
        check_vma=False,
    )
```

profile of v0, /device:TPU:1, one launch (start us, length us, event | category | flops | bytes accessed | tf_op | source)
XLA Modules:
  0.0 813.6 jit_solution(8270312931588945220)
XLA Ops:
  12.2 12.0 %all-to-all-start.2 = ((bf16[32,8,512]{2,1,0:T(8,128)(2,1)}), bf16[32,8,512]{2,1,0:T(8,128)(2,1)S(1)}, u32[]{:S(2)}, u32[]{:S(2)}) async-start(bf16[32,8,512]{2,1,0:T(8,128)(2,1)} %scatter_fusion.2), calls=%async_computation.2 | async-start | bytes 524288 | tf_op jit(solution)/shard_map/all_to_all | solution.py:131
  27.2 8.3 %all-to-all-done.2 = bf16[32,8,512]{2,1,0:T(8,128)(2,1)S(1)} async-done(((bf16[32,8,512]{2,1,0:T(8,128)(2,1)}), bf16[32,8,512]{2,1,0:T(8,128)(2,1)S(1)}, u32[]{:S(2)}, u32[]{:S(2)}) %all-to-all-start.2) | async-done | bytes 262176 | tf_op jit(solution)/shard_map/all_to_all | solution.py:131
  35.5 4.8 all-to-all-start.1
  41.8 2.5 scatter_fusion
  44.3 6.4 all-to-all-done.1
  50.7 4.6 all-to-all-start
  59.8 2.5 scatter_fusion.3
  62.5 41.6 %all-to-all-done = bf16[32,8,4096]{2,1,0:T(8,128)(2,1)S(1)} async-done(((bf16[32,8,4096]{2,1,0:T(8,128)(2,1)}), bf16[32,8,4096]{2,1,0:T(8,128)(2,1)S(1)}, u32[]{:S(2)}, u32[]{:S(2)}) %all-to-all-start) | async-done | bytes 2097184 | tf_op jit(solution)/shard_map/all_to_all | solution.py:129
  104.0 7.1 all-to-all-start.3
  137.9 29.4 %all-to-all-done.3 = bf16[32,8,4096]{2,1,0:T(8,128)(2,1)} async-done(((bf16[32,8,4096]{2,1,0:T(8,128)(2,1)}), bf16[32,8,4096]{2,1,0:T(8,128)(2,1)}, u32[]{:S(2)}, u32[]{:S(2)}) %all-to-all-start.3) | async-done | bytes 2097184 | tf_op jit(solution)/shard_map/all_to_all | solution.py:132
  167.3 2.2 gather_fusion.6
  170.4 2.5 reshape.473
  174.9 2.2 gather_fusion.5
  179.6 2.7 fusion.25
  182.3 53.1 %all-gather.3.cloned.1.call-done = bf16[2048,512]{1,0:T(8,128)(2,1)} async-done(((bf16[64,512]{1,0:T(8,128)(2,1)}), bf16[2048,512]{1,0:T(8,128)(2,1)}) %all-gather.3.cloned.1.call-update) | async-done | bytes 2097168 | tf_op jit(solution)/shard_map/all_gather | solution.py:190
  235.4 2.5 reshape.470
  239.8 2.2 gather_fusion.3
  242.1 2.8 fusion.5
  248.7 28.3 %fusion.23 = f32[2,192,4,128]{3,1,2,0:T(8,128)S(1)} fusion(f32[2,4,192,64,8]{2,3,4,1,0:T(8,128)} %fusion.25, f32[128]{0:T(128)S(1)} %copy-done.32, f32[2,64,4,8]{1,3,2,0:T(8,128)S(1)} %bitcast.232, bf16[1,64,4,8,128]{4,1,3,2,0:T(8,128)(2,1)} %copy.150, bf16[1,64,4,8,128]{4,1,3,2,0:T(8,128)(2,1)} %copy.149, f32[2,4,192,64,8]{2,3,4,1,0:T(8,128)} %copy-done, ...), kind=kOutput, calls=%fused_computation.46 | convolution fusion | flops 212603072 | bytes 8258048 | tf_op jit(solution)/shard_map/ncgqk,nqcgd->nkcd/dot_general | solution.py:74
  277.1 3.3 fusion.20
  284.5 2.5 broadcast.361.clone
  287.0 2.6 scatter_fusion.4
  289.6 3.9 convert_element_type.115
  293.6 2.5 broadcast.361.clone.1
  296.1 2.9 scatter_fusion.5
  299.0 3.8 convert_element_type.120
  305.1 30.2 %fusion.12 = (f32[128]{0:T(128)S(1)}, f32[2,64,4,8]{1,3,2,0:T(8,128)S(1)}, f32[2,64,4,8,128]{4,1,3,2,0:T(8,128)S(1)}) fusion(f32[2,64,4,8]{1,3,2,0:T(8,128)S(1)} %bitcast.233, bf16[1,64,4,8,128]{4,1,3,2,0:T(8,128)(2,1)} %copy.150, bf16[1,64,4,8,128]{4,1,3,2,0:T(8,128)(2,1)} %copy.149, f32[128]{0:T(128)S(1)} %copy-done.33, ...), kind=kOutput, calls=%fused_computation.34 | convolution fusion | flops 216006720 | bytes 9978880 | tf_op jit(solution)/shard_map/ncgqk,nkcd->nqcgd/dot_general | solution.py:71
  336.0 2.6 copy.158
  343.1 3.4 fusion.13
  346.5 159.6 %reduce-scatter.3.cloned.1.call-done = bf16[64,512]{1,0:T(8,128)(2,1)} async-done(((bf16[2048,512]{1,0:T(8,128)(2,1)}), bf16[64,512]{1,0:T(8,128)(2,1)}) %reduce-scatter.3.cloned.1.call-update) | async-done | bytes 65552 | tf_op jit(solution)/shard_map/reduce_scatter | solution.py:226
  508.4 216.5 %reduce-scatter.5.cloned.1.call-done = bf16[64,512]{1,0:T(8,128)(2,1)} async-done(((bf16[2048,512]{1,0:T(8,128)(2,1)}), bf16[64,512]{1,0:T(8,128)(2,1)}) %reduce-scatter.5.cloned.1.call-update) | async-done | bytes 65552 | tf_op jit(solution)/shard_map/reduce_scatter | solution.py:232
  727.5 79.5 %all-reduce = (f32[128]{0:T(128)}, f32[128]{0:T(128)}) all-reduce(f32[128]{0:T(128)S(1)} %get-tuple-element.29, f32[128]{0:T(128)S(1)} %get-tuple-element.31), channel_id=1, replica_groups=mesh['dp'=8,'ctx'=32] {'dp','ctx'}, use_global_device_ids=true, to_apply=%region_22.23 | all-reduce | flops 256 | bytes 2048 | tf_op jit(solution)/shard_map/psum | solution.py:247
  (189 shorter events, 67.9 us)
Async XLA Ops:
  7.2 34.6 %copy-start.9 = (bf16[64,4096]{1,0:T(8,128)(2,1)S(1)}, bf16[64,4096]{1,0:T(8,128)(2,1)}, u32[]{:S(2)}) copy-start(bf16[64,4096]{1,0:T(8,128)(2,1)} %param.22) | copy-start | bytes 1572868
  12.2 23.2 %all-to-all-start.2 = ((bf16[32,8,512]{2,1,0:T(8,128)(2,1)}), bf16[32,8,512]{2,1,0:T(8,128)(2,1)S(1)}, u32[]{:S(2)}, u32[]{:S(2)}) async-start(bf16[32,8,512]{2,1,0:T(8,128)(2,1)} %scatter_fusion.2), calls=%async_computation.2 | async-start | bytes 524288 | tf_op jit(solution)/shard_map/all_to_all | solution.py:131
  35.5 8.8 %copy-start.12 = (bf16[32,8,512]{2,1,0:T(8,128)(2,1)}, bf16[32,8,512]{2,1,0:T(8,128)(2,1)S(1)}, u32[]{:S(2)}) copy-start(bf16[32,8,512]{2,1,0:T(8,128)(2,1)S(1)} %all-to-all-done.2) | copy-start | bytes 786436
  35.5 15.2 %all-to-all-start.1 = ((bf16[32,8,512]{2,1,0:T(8,128)(2,1)}), bf16[32,8,512]{2,1,0:T(8,128)(2,1)S(1)}, u32[]{:S(2)}, u32[]{:S(2)}) async-start(bf16[32,8,512]{2,1,0:T(8,128)(2,1)} %scatter_fusion.1), calls=%async_computation.1 | async-start | bytes 524288 | tf_op jit(solution)/shard_map/all_to_all | solution.py:130
  44.3 11.8 %copy-start.27 = (s32[1,256]{1,0:T(1,128)S(1)}, s32[1,256]{1,0:T(1,128)}, u32[]{:S(2)}) copy-start(s32[1,256]{1,0:T(1,128)} %param.28) | copy-start | bytes 3076
  50.7 53.4 %all-to-all-start = ((bf16[32,8,4096]{2,1,0:T(8,128)(2,1)}), bf16[32,8,4096]{2,1,0:T(8,128)(2,1)S(1)}, u32[]{:S(2)}, u32[]{:S(2)}) async-start(bf16[32,8,4096]{2,1,0:T(8,128)(2,1)} %scatter_fusion), calls=%async_computation | async-start | bytes 4194304 | tf_op jit(solution)/shard_map/all_to_all | solution.py:129
  55.3 4.5 copy-start.10
  55.3 115.1 %all-gather.5.cloned.1.call-start = ((), (), s32[]{:S(2)}) async-start(), calls=%async_computation.7 | async-start | bytes 2162688 | tf_op jit(solution)/shard_map/all_gather | solution.py:191
  62.4 48.8 %copy-start.20 = (bf16[64,512]{1,0:T(8,128)(2,1)S(1)}, bf16[64,512]{1,0:T(8,128)(2,1)}, u32[]{:S(2)}) copy-start(bf16[64,512]{1,0:T(8,128)(2,1)} %param.19) | copy-start | bytes 196612
  62.4 49.7 %copy-start.25 = (f32[128]{0:T(128)S(1)}, f32[128]{0:T(128)}, u32[]{:S(2)}) copy-start(f32[128]{0:T(128)} %param.27) | copy-start | bytes 1540
  62.4 50.6 %copy-start.18 = (bf16[64,512]{1,0:T(8,128)(2,1)S(1)}, bf16[64,512]{1,0:T(8,128)(2,1)}, u32[]{:S(2)}) copy-start(bf16[64,512]{1,0:T(8,128)(2,1)} %param.20) | copy-start | bytes 196612
  62.4 50.6 %copy-start.11 = (bf16[64,4096]{1,0:T(8,128)(2,1)S(1)}, bf16[64,4096]{1,0:T(8,128)(2,1)}, u32[]{:S(2)}) copy-start(bf16[64,4096]{1,0:T(8,128)(2,1)} %param.18) | copy-start | bytes 1572868
  104.0 63.3 %all-to-all-start.3 = ((bf16[32,8,4096]{2,1,0:T(8,128)(2,1)}), bf16[32,8,4096]{2,1,0:T(8,128)(2,1)}, u32[]{:S(2)}, u32[]{:S(2)}) async-start(bf16[32,8,4096]{2,1,0:T(8,128)(2,1)} %scatter_fusion.3), calls=%async_computation.3 | async-start | bytes 4194304 | tf_op jit(solution)/shard_map/all_to_all | solution.py:132
  111.2 124.2 %all-gather.3.cloned.1.call-start = ((), (), s32[]{:S(2)}) async-start(), calls=%async_computation.6 | async-start | bytes 2162688 | tf_op jit(solution)/shard_map/all_gather | solution.py:190
  111.9 6.4 copy-start.29
  112.2 129.8 %copy-start.13 = (bf16[2,64,4,128]{3,1,2,0:T(8,128)(2,1)}, bf16[2,64,4,128]{3,1,2,0:T(8,128)(2,1)S(1)}, u32[]{:S(2)}) copy-start(bf16[2,64,4,128]{3,1,2,0:T(8,128)(2,1)S(1)} %fusion.36) | copy-start | bytes 393220
  113.0 393.2 %reduce-scatter.3.cloned.1.call-start = ((), (), s32[]{:S(2)}) async-start(), calls=%async_computation.8 | async-start | bytes 2162688 | tf_op jit(solution)/shard_map/reduce_scatter | solution.py:226
  132.0 116.7 %copy-start.8 = (f32[2,64,192]{2,1,0:T(8,128)}, f32[2,64,192]{2,1,0:T(8,128)S(1)}, u32[]{:S(2)}) copy-start(f32[2,64,192]{2,1,0:T(8,128)S(1)} %pad_maximum_fusion.3) | copy-start | bytes 294916
  172.9 4.2 copy-start.31
  174.9 4.7 copy-start.14
  174.9 4.7 copy-start.15
  237.9 4.1 copy-start.32
  242.0 2.8 copy-start.17
  244.9 3.9 copy-start.21
  248.7 28.3 %copy-start.2 = (bf16[2,64,4,8,128]{4,3,2,1,0:T(8,128)(2,1)S(1)}, bf16[2,64,4,8,128]{4,3,2,1,0:T(8,128)(2,1)}, u32[]{:S(2)}) copy-start(bf16[2,64,4,8,128]{4,3,2,1,0:T(8,128)(2,1)} %copy-done.1) | copy-start | bytes 3145732
  277.1 27.0 %copy-start.3 = (f32[2,192,4,128]{3,1,2,0:T(8,128)}, f32[2,192,4,128]{3,1,2,0:T(8,128)S(1)}, u32[]{:S(2)}) copy-start(f32[2,192,4,128]{3,1,2,0:T(8,128)S(1)} %fusion.23) | copy-start | bytes 2359300
  284.5 2.5 copy-start.28
  293.5 431.4 %reduce-scatter.5.cloned.1.call-start = ((), (), s32[]{:S(2)}) async-start(), calls=%async_computation.9 | async-start | bytes 2162688 | tf_op jit(solution)/shard_map/reduce_scatter | solution.py:232
  340.4 2.7 copy-start.19
  343.1 163.9 %copy-start.4 = (f32[2,192,4,128]{3,1,2,0:T(8,128)S(1)}, f32[2,192,4,128]{3,1,2,0:T(8,128)}, u32[]{:S(2)}) copy-start(f32[2,192,4,128]{3,1,2,0:T(8,128)} %copy-done.3) | copy-start | bytes 2359300
  343.1 163.9 %slice-start = ((f32[2,192,4,128]{3,1,2,0:T(8,128)}), f32[2,64,4,128]{3,1,2,0:T(8,128)S(1)}, s32[]{:S(2)}) async-start(f32[2,192,4,128]{3,1,2,0:T(8,128)} %copy-done.3), calls=%async_computation.10 | async-start | bytes 524288 | tf_op jit(solution)/shard_map/slice | solution.py:239
  343.1 163.9 %copy-start.26 = (f32[128]{0:T(128)S(1)}, f32[128]{0:T(128)}, u32[]{:S(2)}) copy-start(f32[128]{0:T(128)} %param.27) | copy-start | bytes 1540
  (11 other events, 18.0 us)
Sparse Core Ops, SparseCore 0:
  58.7 101.2 all-gather.4
  162.7 72.6 all-gather.2
  293.7 212.4 reduce-scatter.2
  510.3 214.5 reduce-scatter.4
where the time goes:
time: 815 us; the launch traced here: 814 us
  waiting for transfers between devices  516 us (63%)
  blocking collectives  79.5 us (10%)
  local copies, waits for them, and re-layouts  68.4 us (8%)
  matrix products  67.3 us (8%)
  other arithmetic  39.4 us (5%)
  starting transfers between devices  28.8 us (4%)
  between operations  14.6 us (2%)
    reduce_scatter x1, waiting for transfers between devices, body(): lax.psum_scatter(term_value_rows.reshape(row_count * node, width).astype(...  217 us
    reduce_scatter x1, waiting for transfers between devices, body(): lax.psum_scatter(term_key_rows.reshape(row_count * node, width).astype(jn...  160 us
    psum x1, blocking collectives, body(): q_sum, k_sum = lax.psum((query_norm_term, key_norm_term), ('dp', 'ctx'))  79.5 us
    all_gather x1, waiting for transfers between devices, body(): lax.all_gather(pre_key, 'ctx', axis=0, tiled=True)  53.1 us
    all_to_all x1, waiting for transfers between devices, body(): lax.all_to_all(pack(gen_q), 'ctx', split_axis=0, concat_axis=0, tiled=True)  41.6 us
    dot_general x1, matrix products, attend_grads(): jnp.einsum('ncgqk,nkcd->nqcgd', dscore_bf, keys_bf, preferred_element_typ...  30.2 us
    all_to_all x1, waiting for transfers between devices, body(): lax.all_to_all(pack(gen_cot), 'ctx', split_axis=0, concat_axis=0, tiled=T...  29.4 us
    dot_general x1, matrix products, attend_grads(): jnp.einsum('ncgqk,nqcgd->nkcd', dscore_bf, query_bfloat, preferred_elemen...  28.3 us
  transfers between devices with their start and end apart: 8, of which 7 were waited for; matrix products, arithmetic and copies ran while one was open for 13% of the time, Pallas kernels for 0%

commit v1 on v0

v1 whole, which is shorter than its diff:
```python
import math

import jax
import jax.numpy as jnp
from jax import lax
from jax.experimental import pallas as pl
from jax.experimental.pallas import tpu as pltpu
from jax.sharding import PartitionSpec as P

EPSILON = 1e-06
NZ, NY = 8, 4
N = NZ * NY
BF = jnp.bfloat16
F32 = jnp.float32
MESH = pl.DeviceIdType.MESH
SCALE = 1.0 / math.sqrt(128)


def iota(shape, axis):
    return lax.broadcasted_iota(jnp.int32, shape, axis)


def contract(a, b, da, db):
    return lax.dot_general(a, b, (((da,), (db,)), ((), ())), preferred_element_type=F32)


def inverse_norm(x):
    return lax.rsqrt(jnp.mean(x * x, axis=-1, keepdims=True) + EPSILON)


def norm_back(x, r, gain, upstream):
    scaled = gain * upstream
    inner = jnp.mean(x * scaled, axis=-1, keepdims=True)
    return r * scaled - x * (r * r * r) * inner


def attend(q, cot, gain, keys, vals, mask):
    r = inverse_norm(q)
    qn = (q * r * gain).astype(BF)
    weights = jnp.exp(contract(keys, qn, 1, 1) * SCALE) * mask
    probs = weights * (1.0 / jnp.sum(weights, axis=0, keepdims=True))
    dprob = contract(vals, cot, 1, 1)
    inner = jnp.sum(probs * dprob, axis=0, keepdims=True)
    dscore = (probs * (dprob - inner) * SCALE).astype(BF)
    dq = contract(dscore, keys, 0, 0)
    dk = contract(dscore, qn, 1, 0)
    dv = contract(probs.astype(BF), cot, 1, 0)
    gain_term = jnp.sum(dq * q * r, axis=0, keepdims=True)
    return norm_back(q, r, gain, dq), dk, dv, gain_term


def kernel(
    pre_q, pre_k, pre_v, pre_c, gen_q, gen_k, gen_v, gen_c, qg, kg,
    dest_row, pp_row, bp_row, rew_row, inv_s, pp_s, bp_s, rew_s,
    out_q, out_k, out_v, out_qg, out_kg,
    kv, r1a, s1b, r1b, s2a, r2a, s2b, r2b, t0, rt0, t12, rt12, s4, r4,
    g, rg, gd, rd, m0, m12, dkp, dvp, causal, send, recv, dsend, drecv,
):
    me = lax.axis_index("ctx")
    group = lax.axis_index("dp")
    n_dp = lax.axis_size("dp")

    def peer(k):
        j = k // NY
        dz = jnp.where(j % 2 == 1, (j + 1) // 2, (NZ - j // 2) % NZ)
        return ((me // NY + dz) % NZ) * NY + (me % NY + k % NY) % NY

    def dp_peer(k):
        return (group + k) % n_dp

    def copy(stage, src, dst, target):
        return pltpu.make_async_remote_copy(
            src_ref=src, dst_ref=dst, send_sem=send.at[stage, target], recv_sem=recv.at[stage, me],
            device_id={"ctx": target}, device_id_type=MESH,
        )

    def await_recv(stage, dst, source):
        pltpu.make_async_copy(dst, dst, recv.at[stage, source]).wait()

    def await_send(stage, src, target):
        pltpu.make_async_copy(src, src, send.at[stage, target]).wait()

    def peers(body):
        @pl.loop(1, N)
        def _(k):
            body(peer(k))

    barrier = pltpu.get_barrier_semaphore()

    @pl.loop(1, N)
    def _(k):
        pl.semaphore_signal(barrier, inc=1, device_id={"ctx": peer(k)}, device_id_type=MESH)

    @pl.loop(1, n_dp)
    def _(k):
        pl.semaphore_signal(barrier, inc=1, device_id={"dp": dp_peer(k)}, device_id_type=MESH)

    kgain = kg[...]
    qgain = qg[...]

    for c in range(4):
        x = pre_k[:, c * 128:(c + 1) * 128].astype(F32)
        kv[0, :, c * 128:(c + 1) * 128] = (x * inverse_norm(x) * kgain).astype(BF)
    kv[0, :, 512:] = pre_v[...]
    rows = iota((64, 64), 0)
    spread = (8 * ((rows % 16) // 2) + 2 * (rows // 16) + rows % 2 == iota((64, 64), 1)).astype(F32).astype(BF)
    kv[1, :, :512] = contract(spread, gen_k[...], 1, 0).astype(BF)
    kv[1, :, 512:] = contract(spread, gen_v[...], 1, 0).astype(BF)

    pl.semaphore_wait(barrier, N - 1 + n_dp - 1)

    def fragment(t):
        rb = pl.multiple_of((t // 8) * 16, 16)
        cb = pl.multiple_of((t % 8) * 128, 128)
        return kv.at[:, pl.ds(rb, 16), pl.ds(cb, 128)]

    def send_1a(t):
        copy(0, fragment(t), r1a.at[me], t).start()

    peers(send_1a)
    r1a[me] = fragment(me)[...]

    def slab(t):
        cols = pl.ds(pl.multiple_of(t * 128, 128), 128)
        q = gen_q[:, cols].astype(F32).reshape(8, 8, 128)
        c = gen_c[:, cols].astype(F32).reshape(8, 8, 128)
        return jnp.concatenate([q, c], axis=1).astype(BF)

    def send_1b(t):
        part = s1b.at[pl.ds(t * 8, 8)]
        part[...] = slab(t)
        copy(1, part, r1b.at[pl.ds(me * 8, 8)], t).start()

    peers(send_1b)
    r1b[pl.ds(me * 8, 8)] = slab(me)

    pp = jnp.broadcast_to(pp_row[...].astype(F32), (8, N))
    bp = jnp.broadcast_to(bp_row[...].astype(F32), (8, N))
    pick = (bp_row[...] == iota((N, N), 0)).astype(F32).astype(BF)
    upper = contract(pp.astype(BF), pick, 1, 0)
    spread0 = (iota((N, 512), 0) == iota((N, 512), 1) // 16).astype(F32).astype(BF)
    row0 = (iota((8, 512), 1) % 16).astype(F32)
    spread1 = (iota((N, 1024), 0) == iota((N, 1024), 1) // 32).astype(F32).astype(BF)
    lane1 = iota((8, 1024), 1)
    id0 = contract(pp.astype(BF), spread0, 1, 0) * 16.0 + row0
    parent1 = contract(bp.astype(BF), spread1, 1, 0)
    upper1 = contract(upper.astype(BF), spread1, 1, 0)
    id1 = jnp.where((lane1 // 16) % 2 == 0, parent1, upper1) * 16.0 + (lane1 % 16).astype(F32)
    m0[...] = (iota((512, 512), 0).astype(F32) == id0[:1]).astype(F32).astype(BF)
    m12[...] = (iota((512, 1024), 0).astype(F32) == id1[:1]).astype(F32).astype(BF)
    dest = jnp.broadcast_to(dest_row[...].astype(F32), (8, 256)).astype(BF)
    spread2 = (iota((256, 512), 0) == iota((256, 512), 1) // 2).astype(F32).astype(BF)
    id2 = contract(dest, spread2, 1, 0) * 2.0 + (iota((8, 512), 1) % 2).astype(F32)
    order = (iota((512, 512), 0).astype(F32) == id2[:1]).astype(F32).astype(BF)
    causal[...] = (iota((64, 512), 0) <= iota((64, 512), 1) % 64).astype(F32)

    my_parent = bp_s[0, me]
    my_upper = pp_s[0, my_parent]
    my_above = pp_s[0, me]
    my_root = jnp.where(my_upper >= 0, my_upper, my_parent).astype(F32)
    root = jnp.where(upper >= 0.0, upper, bp)
    member = (root == my_root).astype(F32)
    score = jnp.broadcast_to(rew_row[...].astype(F32), (8, N))
    size = jnp.sum(member, axis=1, keepdims=True)
    center = jnp.sum(member * score, axis=1, keepdims=True) / size
    var = jnp.sum(member * (score - center) ** 2, axis=1, keepdims=True) / size
    adv = ((rew_s[0, me].astype(F32) - center) / jnp.maximum(jnp.sqrt(var), 1.0))[:1]

    peers(lambda t: await_recv(0, r1a.at[t], t))
    s2a[:, 3] = contract(order, r1a[:, 1].reshape(512, 128), 1, 0).astype(BF).reshape(N, 16, 128)

    def fill_2a(t):
        parent = bp_s[0, t]
        s2a[t, 0] = r1a[jnp.maximum(pp_s[0, t], 0), 0]
        s2a[t, 1] = r1a[parent, 0]
        s2a[t, 2] = r1a[jnp.maximum(pp_s[0, parent], 0), 0]

    def send_2a(t):
        fill_2a(t)
        copy(2, s2a.at[t], r2a.at[me], t).start()

    peers(send_2a)
    fill_2a(me)
    r2a[me] = s2a[me]

    peers(lambda t: await_recv(1, r1b.at[pl.ds(t * 8, 8)], t))

    def send_2b(t):
        for p in range(8):
            s2b[t * 8 + p] = r1b[inv_s[0, t * 8 + p]]
        copy(3, s2b.at[pl.ds(t * 8, 8)], r2b.at[pl.ds(me * 8, 8)], t).start()

    peers(send_2b)
    for p in range(8):
        r2b[me * 8 + p] = r1b[inv_s[0, me * 8 + p]]

    def tiles(ref, at, c):
        return jnp.concatenate([ref[8 * b + c] if at is None else ref[8 * b + c, at] for b in range(4)], axis=0)

    peers(lambda t: await_recv(2, r2a.at[t], t))
    g[...] = jnp.zeros((8, 128), F32)
    above = (my_above >= 0).astype(F32)

    @pl.loop(0, 4)
    def _(c):
        col = lambda base, h: pl.ds(pl.multiple_of((base + h) * 128, 128), 128)
        q = jnp.concatenate([pre_q[:, col(8 * c, h)] for h in range(8)], axis=0).astype(F32)
        cot = jnp.concatenate([pre_c[:, col(8 * c, h)] for h in range(8)], axis=0)
        own_k = kv[0, :, col(c, 0)]
        far_k = tiles(r2a, 0, c)
        keys = jnp.concatenate([own_k, far_k], axis=0)
        vals = jnp.concatenate([kv[0, :, col(c, 4)], tiles(r2a, 0, 4 + c)], axis=0)
        mask = jnp.concatenate([causal[...], jnp.full((64, 512), 1.0, F32) * above], axis=0)
        dq, dk, dv, q_term = attend(q, cot, qgain, keys, vals, mask)
        for h in range(8):
            out_q[0:64, col(8 * c, h)] = dq[h * 64:(h + 1) * 64].astype(BF)
        dkp[:, col(c, 0)] = dk[:64]
        dvp[:, col(c, 0)] = dv[:64]
        x = pre_k[:, col(c, 0)].astype(F32)
        k_term = jnp.sum(dk[:64] * x * inverse_norm(x), axis=0, keepdims=True)
        k_term += jnp.sum(dk[64:] * far_k.astype(F32), axis=0, keepdims=True) / kgain
        g[0:1] += q_term
        g[1:2] += k_term
        for b in range(4):
            t0[8 * b + c] = dk[64 + 16 * b:80 + 16 * b].astype(BF)
            t0[8 * b + 4 + c] = dv[64 + 16 * b:80 + 16 * b].astype(BF)

    peers(lambda t: copy(4, t0.at[t], rt0.at[me], t).start())
    rt0[me] = t0[me]

    back = (8 * ((iota((64, 64), 1) % 16) // 2) + 2 * (iota((64, 64), 1) // 16) + iota((64, 64), 1) % 2
            == iota((64, 64), 0)).astype(F32).astype(BF)
    upper_ok = (my_upper >= 0).astype(F32)

    @pl.loop(0, 4)
    def _(step):
        c = (me // 8 + 4 - step) % 4

        @pl.loop(0, 8)
        def _(h):
            @pl.when(8 * c + h != me)
            def _():
                await_recv(3, r2b.at[pl.ds((8 * c + h) * 8, 8)], 8 * c + h)

        col = lambda base, h: pl.ds(pl.multiple_of((base + h) * 128, 128), 128)
        both = r2b[pl.ds(64 * c, 64)].astype(F32)
        q = both[:, :8].reshape(512, 128)
        cot = (both[:, 8:].reshape(512, 128) * adv).astype(BF)
        x = contract(back, tiles(r2a, 3, c), 1, 0)
        r = inverse_norm(x)
        far_k = jnp.concatenate([tiles(r2a, 1, c), tiles(r2a, 2, c)], axis=0)
        keys = jnp.concatenate([(x * r * kgain).astype(BF), far_k], axis=0)
        vals = jnp.concatenate(
            [contract(back, tiles(r2a, 3, 4 + c), 1, 0).astype(BF), tiles(r2a, 1, 4 + c), tiles(r2a, 2, 4 + c)], axis=0
        )
        ones = jnp.full((64, 512), 1.0, F32)
        mask = jnp.concatenate([causal[...], ones, ones * upper_ok], axis=0)
        dq, dk, dv, q_term = attend(q, cot, qgain, keys, vals, mask)
        for h in range(8):
            out_q[64:128, col(8 * c, h)] = dq[h * 64:(h + 1) * 64].astype(BF)
        out_k[64:128, col(c, 0)] = norm_back(x, r, kgain, dk[:64]).astype(BF)
        out_v[64:128, col(c, 0)] = dv[:64].astype(BF)
        k_term = jnp.sum(dk[:64] * x * r, axis=0, keepdims=True)
        k_term += jnp.sum(dk[64:] * far_k.astype(F32), axis=0, keepdims=True) / kgain
        g[0:1] += q_term
        g[1:2] += k_term
        for b in range(4):
            for j in range(2):
                at = 64 + 64 * j + 16 * b
                t12[8 * b + c, j] = dk[at:at + 16].astype(BF)
                t12[8 * b + 4 + c, j] = dv[at:at + 16].astype(BF)

    peers(lambda t: copy(5, t12.at[t], rt12.at[me], t).start())
    rt12[me] = t12[me]
    peers(lambda t: copy(6, g, rg.at[me], t).start())
    rg[me] = g[...]

    peers(lambda t: await_recv(4, rt0.at[t], t))
    total = contract(m0[...], rt0[...].reshape(512, 128), 1, 0)
    peers(lambda t: await_recv(5, rt12.at[t], t))
    total += contract(m12[...], rt12[...].reshape(1024, 128), 1, 0)
    s4[...] = total.astype(BF).reshape(N, 16, 128)
    peers(lambda t: copy(7, s4.at[t], r4.at[me], t).start())
    r4[me] = s4[me]

    peers(lambda t: await_recv(6, rg.at[t], t))
    gd[...] = jnp.sum(rg[...], axis=0)

    def dp_copy(k):
        t = dp_peer(k)
        return pltpu.make_async_remote_copy(
            src_ref=gd, dst_ref=rd.at[group], send_sem=dsend.at[t], recv_sem=drecv.at[group],
            device_id={"dp": t}, device_id_type=MESH,
        )

    @pl.loop(1, n_dp)
    def _(k):
        dp_copy(k).start()

    rd[group] = gd[...]

    peers(lambda t: await_recv(7, r4.at[t], t))
    for c in range(4):
        cols = slice(c * 128, (c + 1) * 128)
        x = pre_k[:, cols].astype(F32)
        dk = dkp[:, cols] + tiles(r4, None, c).astype(F32)
        out_k[0:64, cols] = norm_back(x, inverse_norm(x), kgain, dk).astype(BF)
        out_v[0:64, cols] = (dvp[:, cols] + tiles(r4, None, 4 + c).astype(F32)).astype(BF)

    @pl.loop(1, n_dp)
    def _(k):
        t = dp_peer(k)
        pltpu.make_async_copy(rd.at[t], rd.at[t], drecv.at[t]).wait()

    sums = jnp.sum(rd[...], axis=0)
    out_qg[...] = sums[0:1]
    out_kg[...] = sums[1:2]

    def drain(t):
        await_send(0, fragment(t), t)
        await_send(1, s1b.at[pl.ds(t * 8, 8)], t)
        await_send(2, s2a.at[t], t)
        await_send(3, s2b.at[pl.ds(t * 8, 8)], t)
        await_send(4, t0.at[t], t)
        await_send(5, t12.at[t], t)
        await_send(6, g, t)
        await_send(7, s4.at[t], t)

    peers(drain)

    @pl.loop(1, n_dp)
    def _(k):
        t = dp_peer(k)
        pltpu.make_async_copy(gd, gd, dsend.at[t]).wait()


def body(
    pre_q, prefix_keys, prefix_values, pre_cot, gen_q, rollout_keys, rollout_values, gen_cot,
    q_gain, k_gain, piece_dest, prefix_parent, branch_parent, rewards,
):
    n_dp = lax.axis_size("dp")
    piece = jnp.arange(256, dtype=jnp.int32)
    inverse = jnp.sum(
        jnp.where(piece_dest[0][:, None] == piece[None, :], piece[:, None], 0), axis=0, dtype=jnp.int32
    )[None]
    vmem = pl.BlockSpec(memory_space=pltpu.VMEM)
    smem = pl.BlockSpec(memory_space=pltpu.SMEM)
    out_q, out_k, out_v, out_qg, out_kg = pl.pallas_call(
        kernel,
        out_shape=(
            jax.ShapeDtypeStruct((128, 4096), BF),
            jax.ShapeDtypeStruct((128, 512), BF),
            jax.ShapeDtypeStruct((128, 512), BF),
            jax.ShapeDtypeStruct((1, 128), F32),
            jax.ShapeDtypeStruct((1, 128), F32),
        ),
        in_specs=[vmem] * 14 + [smem] * 4,
        out_specs=[vmem] * 5,
        scratch_shapes=[
            pltpu.VMEM((2, 64, 1024), BF),
            pltpu.VMEM((N, 2, 16, 128), BF),
            pltpu.VMEM((256, 16, 128), BF),
            pltpu.VMEM((256, 16, 128), BF),
            pltpu.VMEM((N, 4, 16, 128), BF),
            pltpu.VMEM((N, 4, 16, 128), BF),
            pltpu.VMEM((256, 16, 128), BF),
            pltpu.VMEM((256, 16, 128), BF),
            pltpu.VMEM((N, 16, 128), BF),
            pltpu.VMEM((N, 16, 128), BF),
            pltpu.VMEM((N, 2, 16, 128), BF),
            pltpu.VMEM((N, 2, 16, 128), BF),
            pltpu.VMEM((N, 16, 128), BF),
            pltpu.VMEM((N, 16, 128), BF),
            pltpu.VMEM((8, 128), F32),
            pltpu.VMEM((N, 8, 128), F32),
            pltpu.VMEM((8, 128), F32),
            pltpu.VMEM((n_dp, 8, 128), F32),
            pltpu.VMEM((512, 512), BF),
            pltpu.VMEM((512, 1024), BF),
            pltpu.VMEM((64, 512), F32),
            pltpu.VMEM((64, 512), F32),
            pltpu.VMEM((64, 512), F32),
            pltpu.SemaphoreType.DMA((8, N)),
            pltpu.SemaphoreType.DMA((8, N)),
            pltpu.SemaphoreType.DMA((n_dp,)),
            pltpu.SemaphoreType.DMA((n_dp,)),
        ],
        compiler_params=pltpu.CompilerParams(
            collective_id=0, has_side_effects=True, vmem_limit_bytes=40 * 1024 * 1024
        ),
    )(
        pre_q, prefix_keys, prefix_values, pre_cot, gen_q, rollout_keys, rollout_values, gen_cot,
        q_gain.reshape(1, 128), k_gain.reshape(1, 128),
        piece_dest, prefix_parent, branch_parent, rewards,
        inverse, prefix_parent, branch_parent, rewards,
    )
    return out_q, out_k, out_v, out_qg.reshape(128), out_kg.reshape(128)


def solution(mesh):
    rows = P(("dp", "ctx"), None)
    return jax.shard_map(
        body,
        mesh=mesh,
        in_specs=(rows,) * 8 + (P(), P()) + (P("dp", None),) * 4,
        out_specs=(rows, rows, rows, P(), P()),
        check_vma=False,
    )
```

time: 815 us -> 118 us (0.14)
  waiting for transfers between devices: 516 us -> 0 us
  Pallas kernels: 0 us -> 104 us
  blocking collectives: 79.5 us -> 0 us
  matrix products: 67.3 us -> 0 us
  local copies, waits for them, and re-layouts: 68.4 us -> 12.2 us
  other arithmetic: 39.4 us -> 0.11 us
  starting transfers between devices: 28.8 us -> 0 us
  between operations: 14.6 us -> 0.69 us
    reduce_scatter x2 -> x0, waiting for transfers between devices: 376 us -> none  [the longest x1 217 us: body(): lax.psum_scatter(term_value_rows.reshape(row_count * node, width).astype(...]
    pallas_call x0 -> x1, Pallas kernels: none -> 104 us  [body(): pl.pallas_call(kernel, out_shape=(jax.ShapeDtypeStruct((128, 4096), BF),...]
    all_to_all x4 -> x0, waiting for transfers between devices: 85.7 us -> none  [the longest x1 41.6 us: body(): lax.all_to_all(pack(gen_q), 'ctx', split_axis=0, concat_axis=0, tiled=True)]
    psum x1 -> x0, blocking collectives: 79.5 us -> none  [body(): q_sum, k_sum = lax.psum((query_norm_term, key_norm_term), ('dp', 'ctx'))]
    dot_general x5 -> x0, matrix products: 67.3 us -> none  [the longest x1 30.2 us: attend_grads(): jnp.einsum('ncgqk,nkcd->nqcgd', dscore_bf, keys_bf, preferred_element_typ...]
    all_gather x2 -> x0, waiting for transfers between devices: 53.1 us -> none  [the longest x1 53.1 us: body(): lax.all_gather(pre_key, 'ctx', axis=0, tiled=True)]
    all_to_all x4 -> x0, starting transfers between devices: 28.6 us -> none  [the longest x1 12 us: body(): lax.all_to_all(pack(rollout_values), 'ctx', split_axis=0, concat_axis=0,...]
    convert_element_type x10 -> x0, other arithmetic: 16.2 us -> none  [the longest x1 3.86 us: body(): term_key_rows.reshape(row_count * node, width).astype(jnp.bfloat16)]
  transfers between devices with their start and end apart: 8 -> 0, of which waited for: 7 -> 0; matrix products, arithmetic and copies ran while one was open for 13% -> 0% of each run, Pallas kernels for 0% -> 0%
where the time goes in v1:
time: 118 us; the launch traced here: 117 us
  Pallas kernels  104 us (88%)
  local copies, waits for them, and re-layouts  12.2 us (10%)
    pallas_call x1, Pallas kernels, body(): pl.pallas_call(kernel, out_shape=(jax.ShapeDtypeStruct((128, 4096), BF),...  104 us
    unnamed x33, local copies, waits for them, and re-layouts  12.2 us

profile of v1, /device:TPU:1, one launch (start us, length us, event | category | flops | bytes accessed | tf_op | source)
XLA Modules:
  0.0 117.0 jit_solution(16215916722373684979)
XLA Ops:
  0.6 0.0 copy-start.8
  0.6 0.7 copy-done.8
  1.3 0.0 copy-start.12
  1.3 0.0 copy-start.13
  1.3 0.1 select_reduce_fusion
  1.4 0.0 copy-start.9
  1.4 0.0 copy-start.10
  1.5 0.0 copy-start.11
  1.5 0.5 copy-done.12
  2.0 0.0 copy-done.13
  2.0 0.1 copy-done.9
  2.1 0.0 copy-done.10
  2.1 0.0 copy-done.11
  2.1 0.0 copy-start
  2.1 1.0 copy-done
  3.2 0.0 copy-start.1
  3.2 1.0 copy-done.1
  4.2 0.0 copy-start.2
  4.2 1.0 copy-done.2
  5.2 0.0 copy-start.3
  5.3 1.0 copy-done.3
  6.3 0.0 copy-start.4
  6.3 0.8 copy-done.4
  7.1 0.8 copy-done.5
  8.0 0.8 copy-done.6
  8.8 0.8 copy-done.7
  9.7 104.0 %shard_map.173 = (bf16[128,4096]{1,0:T(8,128)(2,1)S(1)}, bf16[128,512]{1,0:T(8,128)(2,1)S(1)}, bf16[128,512]{1,0:T(8,128)(2,1)S(1)}, f32[1,128]{1,0:T(1,128)S(1)}, f32[1,128]{1,0:T(1,128)S(1)}) custom-call(bf16[64,4096]{1,0:T(8,128)(2,1)S(1)} %copy-done, bf16[64,512]{1,0:T(8,128)(2,1)S(1)} %copy-done.4, bf16[64,512]{1,0:T(8,128)(2,1)S(1)} %copy-done.5, ...), custom_call_target="tpu_custom_call" | custom-call | tf_op jit(solution)/shard_map/pallas_call | solution.py:348
  113.6 1.0 copy.24
  114.6 0.7 copy.25
  115.3 0.7 copy.26
  115.9 0.5 copy.27
  116.4 0.5 copy.28
  (3 shorter events, 0.0 us)
Async XLA Ops:
  0.6 0.7 copy-start.8
  1.3 0.7 copy-start.12
  1.3 0.7 copy-start.13
  1.4 0.7 copy-start.9
  1.4 0.7 copy-start.10
  1.5 0.7 copy-start.11
  2.1 1.0 copy-start
  3.2 1.0 copy-start.1
  4.2 1.0 copy-start.2
  5.2 1.0 copy-start.3
  6.3 0.8 copy-start.4
  7.1 0.8 copy-start.5
  8.0 0.8 copy-start.6
  8.8 0.8 copy-start.7

commit v2 on v1

--- a/solution.py
+++ b/solution.py
@@ -49,13 +49,20 @@
     return norm_back(q, r, gain, dq), dk, dv, gain_term
 
 
-def kernel(
-    pre_q, pre_k, pre_v, pre_c, gen_q, gen_k, gen_v, gen_c, qg, kg,
-    dest_row, pp_row, bp_row, rew_row, inv_s, pp_s, bp_s, rew_s,
-    out_q, out_k, out_v, out_qg, out_kg,
-    kv, r1a, s1b, r1b, s2a, r2a, s2b, r2b, t0, rt0, t12, rt12, s4, r4,
+def kernel(*refs):
+    ins, outs, rest = refs[:14], refs[14:19], refs[19:]
+    held, small, (table, loaded, indexed) = rest[:14], rest[14:18], rest[18:21]
+    compute(ins, outs, rest[21:26], held, small, table, loaded, indexed, *rest[26:])
+
+
+def compute(
+    ins, outs, staged, held, small, table, loaded, indexed,
+    stored, kv, r1a, s1b, r1b, s2a, r2a, s2b, r2b, t0, rt0, t12, rt12, s4, r4,
     g, rg, gd, rd, m0, m12, dkp, dvp, causal, send, recv, dsend, drecv,
 ):
+    pre_q, pre_k, pre_v, pre_c, gen_q, gen_k, gen_v, gen_c, qg, kg, dest_row, pp_row, bp_row, rew_row = held
+    inv_s, pp_s, bp_s, rew_s = small
+    out_q, out_k, out_v, out_qg, out_kg = staged
     me = lax.axis_index("ctx")
     group = lax.axis_index("dp")
     n_dp = lax.axis_size("dp")
@@ -85,6 +92,19 @@
         def _(k):
             body(peer(k))
 
+    def store(i, output, rows):
+        return pltpu.make_async_copy(staged[output].at[rows], outs[output].at[rows], stored.at[i])
+
+    upper_half, lower_half = pl.ds(0, 64), pl.ds(64, 64)
+    stores = [
+        store(0, 0, upper_half), store(1, 1, lower_half), store(2, 2, lower_half),
+        store(3, 1, upper_half), store(4, 2, upper_half), store(5, 3, pl.ds(0, 1)), store(6, 4, pl.ds(0, 1)),
+    ]
+
+    def store_branch(c):
+        at = (lower_half, pl.ds(pl.multiple_of(1024 * c, 128), 1024))
+        return pltpu.make_async_copy(staged[0].at[at], outs[0].at[at], stored.at[7 + c])
+
     barrier = pltpu.get_barrier_semaphore()
 
     @pl.loop(1, N)
@@ -94,6 +114,13 @@
     @pl.loop(1, n_dp)
     def _(k):
         pl.semaphore_signal(barrier, inc=1, device_id={"dp": dp_peer(k)}, device_id_type=MESH)
+
+    fetch = [pltpu.make_async_copy(ins[i], held[i], loaded.at[i]) for i in range(14)]
+    fetch += [pltpu.make_async_copy(ins[i], small[i - 10], indexed.at[i - 10]) for i in (11, 12, 13)]
+    for i in (8, 9, 1, 2, 5, 6, 4, 7, 10, 11, 12, 13, 14, 15, 16, 0, 3):
+        fetch[i].start()
+    for i in (8, 9, 1, 2, 5, 6):
+        fetch[i].wait()
 
     kgain = kg[...]
     qgain = qg[...]
@@ -107,6 +134,8 @@
     kv[1, :, :512] = contract(spread, gen_k[...], 1, 0).astype(BF)
     kv[1, :, 512:] = contract(spread, gen_v[...], 1, 0).astype(BF)
 
+    for i in (4, 7):
+        fetch[i].wait()
     pl.semaphore_wait(barrier, N - 1 + n_dp - 1)
 
     def fragment(t):
@@ -134,6 +163,14 @@
     peers(send_1b)
     r1b[pl.ds(me * 8, 8)] = slab(me)
 
+    for i in (10, 11, 12, 13, 14, 15, 16):
+        fetch[i].wait()
+    column = jnp.broadcast_to(dest_row[...], (128, 256)).T
+    for half in range(2):
+        hit = column == iota((256, 128), 1) + 128 * half
+        table[:, half * 128:(half + 1) * 128] = jnp.max(jnp.where(hit, iota((256, 128), 0), 0), axis=0, keepdims=True)
+    lookup = pltpu.make_async_copy(table, inv_s, indexed.at[0])
+    lookup.start()
     pp = jnp.broadcast_to(pp_row[...].astype(F32), (8, N))
     bp = jnp.broadcast_to(bp_row[...].astype(F32), (8, N))
     pick = (bp_row[...] == iota((N, N), 0)).astype(F32).astype(BF)
@@ -183,6 +220,7 @@
     fill_2a(me)
     r2a[me] = s2a[me]
 
+    lookup.wait()
     peers(lambda t: await_recv(1, r1b.at[pl.ds(t * 8, 8)], t))
 
     def send_2b(t):
@@ -197,6 +235,8 @@
     def tiles(ref, at, c):
         return jnp.concatenate([ref[8 * b + c] if at is None else ref[8 * b + c, at] for b in range(4)], axis=0)
 
+    for i in (0, 3):
+        fetch[i].wait()
     peers(lambda t: await_recv(2, r2a.at[t], t))
     g[...] = jnp.zeros((8, 128), F32)
     above = (my_above >= 0).astype(F32)
@@ -225,8 +265,16 @@
             t0[8 * b + c] = dk[64 + 16 * b:80 + 16 * b].astype(BF)
             t0[8 * b + 4 + c] = dv[64 + 16 * b:80 + 16 * b].astype(BF)
 
+    stores[0].start()
     peers(lambda t: copy(4, t0.at[t], rt0.at[me], t).start())
     rt0[me] = t0[me]
+
+    def drain_early(t):
+        await_send(0, fragment(t), t)
+        await_send(1, s1b.at[pl.ds(t * 8, 8)], t)
+        await_send(2, s2a.at[t], t)
+
+    peers(drain_early)
 
     back = (8 * ((iota((64, 64), 1) % 16) // 2) + 2 * (iota((64, 64), 1) // 16) + iota((64, 64), 1) % 2
             == iota((64, 64), 0)).astype(F32).astype(BF)
@@ -234,7 +282,7 @@
 
     @pl.loop(0, 4)
     def _(step):
-        c = (me // 8 + 4 - step) % 4
+        c = (me // 8 + jnp.where(step < 2, step, 5 - step)) % 4
 
         @pl.loop(0, 8)
         def _(h):
@@ -269,14 +317,28 @@
                 at = 64 + 64 * j + 16 * b
                 t12[8 * b + c, j] = dk[at:at + 16].astype(BF)
                 t12[8 * b + 4 + c, j] = dv[at:at + 16].astype(BF)
-
-    peers(lambda t: copy(5, t12.at[t], rt12.at[me], t).start())
+        store_branch(c).start()
+        for b in range(8):
+            t = 4 * b + c
+
+            @pl.when(t != me)
+            def _():
+                copy(5, t12.at[t], rt12.at[me], t).start()
+
     rt12[me] = t12[me]
+    stores[1].start()
+    stores[2].start()
     peers(lambda t: copy(6, g, rg.at[me], t).start())
     rg[me] = g[...]
 
     peers(lambda t: await_recv(4, rt0.at[t], t))
     total = contract(m0[...], rt0[...].reshape(512, 128), 1, 0)
+
+    def drain_later(t):
+        await_send(3, s2b.at[pl.ds(t * 8, 8)], t)
+        await_send(4, t0.at[t], t)
+
+    peers(drain_later)
     peers(lambda t: await_recv(5, rt12.at[t], t))
     total += contract(m12[...], rt12[...].reshape(1024, 128), 1, 0)
     s4[...] = total.astype(BF).reshape(N, 16, 128)
@@ -307,6 +369,9 @@
         out_k[0:64, cols] = norm_back(x, inverse_norm(x), kgain, dk).astype(BF)
         out_v[0:64, cols] = (dvp[:, cols] + tiles(r4, None, 4 + c).astype(F32)).astype(BF)
 
+    stores[3].start()
+    stores[4].start()
+
     @pl.loop(1, n_dp)
     def _(k):
         t = dp_peer(k)
@@ -315,13 +380,10 @@
     sums = jnp.sum(rd[...], axis=0)
     out_qg[...] = sums[0:1]
     out_kg[...] = sums[1:2]
+    stores[5].start()
+    stores[6].start()
 
     def drain(t):
-        await_send(0, fragment(t), t)
-        await_send(1, s1b.at[pl.ds(t * 8, 8)], t)
-        await_send(2, s2a.at[t], t)
-        await_send(3, s2b.at[pl.ds(t * 8, 8)], t)
-        await_send(4, t0.at[t], t)
         await_send(5, t12.at[t], t)
         await_send(6, g, t)
         await_send(7, s4.at[t], t)
@@ -332,6 +394,29 @@
     def _(k):
         t = dp_peer(k)
         pltpu.make_async_copy(gd, gd, dsend.at[t]).wait()
+
+    for each in stores:
+        each.wait()
+
+    @pl.loop(0, 4)
+    def _(c):
+        store_branch(c).wait()
+
+
+def write_out(*refs):
+    src, dst, mid = refs[:5], refs[5:10], refs[10:15]
+    loads, stores = refs[15:]
+    chunks = [(0, pl.ds(32 * i, 32)) for i in range(4)] + [(1, pl.ds(0, 128)), (2, pl.ds(0, 128))]
+    chunks += [(3, pl.ds(0, 1)), (4, pl.ds(0, 1))]
+    load = [pltpu.make_async_copy(src[a].at[r], mid[a].at[r], loads.at[n]) for n, (a, r) in enumerate(chunks)]
+    store = [pltpu.make_async_copy(mid[a].at[r], dst[a].at[r], stores.at[n]) for n, (a, r) in enumerate(chunks)]
+    for each in load:
+        each.start()
+    for first, then in zip(load, store):
+        first.wait()
+        then.start()
+    for each in store:
+        each.wait()
 
 
 def body(
@@ -339,12 +424,7 @@
     q_gain, k_gain, piece_dest, prefix_parent, branch_parent, rewards,
 ):
     n_dp = lax.axis_size("dp")
-    piece = jnp.arange(256, dtype=jnp.int32)
-    inverse = jnp.sum(
-        jnp.where(piece_dest[0][:, None] == piece[None, :], piece[:, None], 0), axis=0, dtype=jnp.int32
-    )[None]
-    vmem = pl.BlockSpec(memory_space=pltpu.VMEM)
-    smem = pl.BlockSpec(memory_space=pltpu.SMEM)
+    hbm = pl.BlockSpec(memory_space=pl.ANY)
     out_q, out_k, out_v, out_qg, out_kg = pl.pallas_call(
         kernel,
         out_shape=(
@@ -354,9 +434,36 @@
             jax.ShapeDtypeStruct((1, 128), F32),
             jax.ShapeDtypeStruct((1, 128), F32),
         ),
-        in_specs=[vmem] * 14 + [smem] * 4,
-        out_specs=[vmem] * 5,
+        in_specs=[hbm] * 14,
+        out_specs=[hbm] * 5,
         scratch_shapes=[
+            pltpu.VMEM((64, 4096), BF),
+            pltpu.VMEM((64, 512), BF),
+            pltpu.VMEM((64, 512), BF),
+            pltpu.VMEM((64, 4096), BF),
+            pltpu.VMEM((64, 4096), BF),
+            pltpu.VMEM((64, 512), BF),
+            pltpu.VMEM((64, 512), BF),
+            pltpu.VMEM((64, 4096), BF),
+            pltpu.VMEM((1, 128), F32),
+            pltpu.VMEM((1, 128), F32),
+            pltpu.VMEM((1, 256), jnp.int32),
+            pltpu.VMEM((1, N), jnp.int32),
+            pltpu.VMEM((1, N), jnp.int32),
+            pltpu.VMEM((1, N), jnp.int32),
+            pltpu.SMEM((1, 256), jnp.int32),
+            pltpu.SMEM((1, N), jnp.int32),
+            pltpu.SMEM((1, N), jnp.int32),
+            pltpu.SMEM((1, N), jnp.int32),
+            pltpu.VMEM((1, 256), jnp.int32),
+            pltpu.SemaphoreType.DMA((14,)),
+            pltpu.SemaphoreType.DMA((4,)),
+            pltpu.VMEM((128, 4096), BF),
+            pltpu.VMEM((128, 512), BF),
+            pltpu.VMEM((128, 512), BF),
+            pltpu.VMEM((1, 128), F32),
+            pltpu.VMEM((1, 128), F32),
+            pltpu.SemaphoreType.DMA((11,)),
             pltpu.VMEM((2, 64, 1024), BF),
             pltpu.VMEM((N, 2, 16, 128), BF),
             pltpu.VMEM((256, 16, 128), BF),
@@ -386,14 +493,22 @@
             pltpu.SemaphoreType.DMA((n_dp,)),
         ],
         compiler_params=pltpu.CompilerParams(
-            collective_id=0, has_side_effects=True, vmem_limit_bytes=40 * 1024 * 1024
+            collective_id=0, has_side_effects=True, vmem_limit_bytes=60 * 1024 * 1024
         ),
     )(
         pre_q, prefix_keys, prefix_values, pre_cot, gen_q, rollout_keys, rollout_values, gen_cot,
         q_gain.reshape(1, 128), k_gain.reshape(1, 128),
         piece_dest, prefix_parent, branch_parent, rewards,
-        inverse, prefix_parent, branch_parent, rewards,
     )
+    results = (out_q, out_k, out_v, out_qg, out_kg)
+    out_q, out_k, out_v, out_qg, out_kg = pl.pallas_call(
+        write_out,
+        out_shape=tuple(jax.ShapeDtypeStruct(x.shape, x.dtype) for x in results),
+        in_specs=[hbm] * 5,
+        out_specs=[hbm] * 5,
+        scratch_shapes=[pltpu.VMEM(x.shape, x.dtype) for x in results]
+        + [pltpu.SemaphoreType.DMA((8,)), pltpu.SemaphoreType.DMA((8,))],
+    )(*results)
     return out_q, out_k, out_v, out_qg.reshape(128), out_kg.reshape(128)
 
 

time: 118 us -> 105 us (0.89)
  local copies, waits for them, and re-layouts: 12.2 us -> 0 us
    unnamed x33 -> x0, local copies, waits for them, and re-layouts: 12.2 us -> none
    pallas_call x1, Pallas kernels: 104 us -> 101 us  [body(): pl.pallas_call(kernel, out_shape=(jax.ShapeDtypeStruct((128, 4096), BF),...]
    pallas_call x0 -> x1, Pallas kernels: none -> 2.14 us  [body(): pl.pallas_call(write_out, out_shape=tuple((jax.ShapeDtypeStruct(x.shape,...]
where the time goes in v2:
time: 105 us; the launch traced here: 103 us
  Pallas kernels  103 us (98%)
    pallas_call x1, Pallas kernels, body(): pl.pallas_call(kernel, out_shape=(jax.ShapeDtypeStruct((128, 4096), BF),...  101 us
    pallas_call x1, Pallas kernels, body(): pl.pallas_call(write_out, out_shape=tuple((jax.ShapeDtypeStruct(x.shape,...  2.14 us

profile of v2, /device:TPU:1, one launch (start us, length us, event | category | flops | bytes accessed | tf_op | source)
XLA Modules:
  0.0 103.5 jit_solution(15640842214191767698)
XLA Ops:
  0.6 100.7 %shard_map.173 = (bf16[128,4096]{1,0:T(8,128)(2,1)}, bf16[128,512]{1,0:T(8,128)(2,1)}, bf16[128,512]{1,0:T(8,128)(2,1)}, f32[1,128]{1,0:T(1,128)}, f32[1,128]{1,0:T(1,128)}) custom-call(bf16[64,4096]{1,0:T(8,128)(2,1)} %refs_0_.1, bf16[64,512]{1,0:T(8,128)(2,1)} %refs_1_.1, bf16[64,512]{1,0:T(8,128)(2,1)} %refs_2_.1, bf16[64,4096]{1,0:T(8,128)(2,1)} %refs_3_.1, ...), custom_call_target="tpu_custom_call" | custom-call | tf_op jit(solution)/shard_map/pallas_call | solution.py:428
  101.4 2.1 %shard_map.174 = (bf16[128,4096]{1,0:T(8,128)(2,1)}, bf16[128,512]{1,0:T(8,128)(2,1)}, bf16[128,512]{1,0:T(8,128)(2,1)}, f32[1,128]{1,0:T(1,128)}, f32[1,128]{1,0:T(1,128)}) custom-call(bf16[128,4096]{1,0:T(8,128)(2,1)} %get-tuple-element.15.refs_0_, bf16[128,512]{1,0:T(8,128)(2,1)} %get-tuple-element.16.refs_1_, ...), custom_call_target="tpu_custom_call" | custom-call | tf_op jit(solution)/shard_map/pallas_call | solution.py:504

commit v3 on v2

--- a/solution.py
+++ b/solution.py
@@ -58,7 +58,7 @@
 def compute(
     ins, outs, staged, held, small, table, loaded, indexed,
     stored, kv, r1a, s1b, r1b, s2a, r2a, s2b, r2b, t0, rt0, t12, rt12, s4, r4,
-    g, rg, gd, rd, m0, m12, dkp, dvp, causal, send, recv, dsend, drecv,
+    g, rg, gd, rd, m0, m12, dkp, dvp, causal, send, recv, dsem,
 ):
     pre_q, pre_k, pre_v, pre_c, gen_q, gen_k, gen_v, gen_c, qg, kg, dest_row, pp_row, bp_row, rew_row = held
     inv_s, pp_s, bp_s, rew_s = small
@@ -68,29 +68,31 @@
     n_dp = lax.axis_size("dp")
 
     def peer(k):
-        j = k // NY
-        dz = jnp.where(j % 2 == 1, (j + 1) // 2, (NZ - j // 2) % NZ)
-        return ((me // NY + dz) % NZ) * NY + (me % NY + k % NY) % NY
+        j, m = lax.div(k, NY), lax.rem(k, NY)
+        dz = NZ + NZ // 2 + lax.div(j + 1, 2) * (1 - 2 * lax.rem(j, 2))
+        dy = NY + NY // 2 + lax.div(m + 1, 2) * (1 - 2 * lax.rem(m, 2))
+        return lax.rem(lax.div(me, NY) + dz, NZ) * NY + lax.rem(me + dy, NY)
 
     def dp_peer(k):
-        return (group + k) % n_dp
+        return lax.rem(group + k, n_dp)
 
     def copy(stage, src, dst, target):
+        arrived = recv.at[8 + lax.div(me, 8)] if stage == 3 else recv.at[stage]
         return pltpu.make_async_remote_copy(
-            src_ref=src, dst_ref=dst, send_sem=send.at[stage, target], recv_sem=recv.at[stage, me],
+            src_ref=src, dst_ref=dst, send_sem=send.at[stage], recv_sem=arrived,
             device_id={"ctx": target}, device_id_type=MESH,
         )
 
-    def await_recv(stage, dst, source):
-        pltpu.make_async_copy(dst, dst, recv.at[stage, source]).wait()
-
-    def await_send(stage, src, target):
-        pltpu.make_async_copy(src, src, send.at[stage, target]).wait()
+    def await_all(sem, ref):
+        pltpu.make_async_copy(ref, ref, sem).wait()
 
     def peers(body):
-        @pl.loop(1, N)
+        @pl.loop(0, N - 1)
         def _(k):
             body(peer(k))
+
+    def others(ref, size=1):
+        return ref.at[pl.ds(0, (N - 1) * size)]
 
     def store(i, output, rows):
         return pltpu.make_async_copy(staged[output].at[rows], outs[output].at[rows], stored.at[i])
@@ -107,9 +109,10 @@
 
     barrier = pltpu.get_barrier_semaphore()
 
-    @pl.loop(1, N)
-    def _(k):
-        pl.semaphore_signal(barrier, inc=1, device_id={"ctx": peer(k)}, device_id_type=MESH)
+    def greet(t):
+        pl.semaphore_signal(barrier, inc=1, device_id={"ctx": t}, device_id_type=MESH)
+
+    peers(greet)
 
     @pl.loop(1, n_dp)
     def _(k):
@@ -117,13 +120,12 @@
 
     fetch = [pltpu.make_async_copy(ins[i], held[i], loaded.at[i]) for i in range(14)]
     fetch += [pltpu.make_async_copy(ins[i], small[i - 10], indexed.at[i - 10]) for i in (11, 12, 13)]
-    for i in (8, 9, 1, 2, 5, 6, 4, 7, 10, 11, 12, 13, 14, 15, 16, 0, 3):
+    for i in (9, 1, 2, 5, 6, 4, 7, 10, 11, 12, 13, 14, 15, 16, 8):
         fetch[i].start()
-    for i in (8, 9, 1, 2, 5, 6):
+    for i in (9, 1, 2, 5, 6):
         fetch[i].wait()
 
     kgain = kg[...]
-    qgain = qg[...]
 
     for c in range(4):
         x = pre_k[:, c * 128:(c + 1) * 128].astype(F32)
@@ -163,8 +165,11 @@
     peers(send_1b)
     r1b[pl.ds(me * 8, 8)] = slab(me)
 
-    for i in (10, 11, 12, 13, 14, 15, 16):
+    for i in (8, 10, 11, 12, 13, 14, 15, 16):
         fetch[i].wait()
+    qgain = qg[...]
+    for i in (0, 3):
+        fetch[i].start()
     column = jnp.broadcast_to(dest_row[...], (128, 256)).T
     for half in range(2):
         hit = column == iota((256, 128), 1) + 128 * half
@@ -203,7 +208,7 @@
     var = jnp.sum(member * (score - center) ** 2, axis=1, keepdims=True) / size
     adv = ((rew_s[0, me].astype(F32) - center) / jnp.maximum(jnp.sqrt(var), 1.0))[:1]
 
-    peers(lambda t: await_recv(0, r1a.at[t], t))
+    await_all(recv.at[0], others(r1a))
     s2a[:, 3] = contract(order, r1a[:, 1].reshape(512, 128), 1, 0).astype(BF).reshape(N, 16, 128)
 
     def fill_2a(t):
@@ -221,7 +226,7 @@
     r2a[me] = s2a[me]
 
     lookup.wait()
-    peers(lambda t: await_recv(1, r1b.at[pl.ds(t * 8, 8)], t))
+    await_all(recv.at[1], others(r1b, 8))
 
     def send_2b(t):
         for p in range(8):
@@ -237,7 +242,7 @@
 
     for i in (0, 3):
         fetch[i].wait()
-    peers(lambda t: await_recv(2, r2a.at[t], t))
+    await_all(recv.at[2], others(r2a))
     g[...] = jnp.zeros((8, 128), F32)
     above = (my_above >= 0).astype(F32)
 
@@ -269,12 +274,9 @@
     peers(lambda t: copy(4, t0.at[t], rt0.at[me], t).start())
     rt0[me] = t0[me]
 
-    def drain_early(t):
-        await_send(0, fragment(t), t)
-        await_send(1, s1b.at[pl.ds(t * 8, 8)], t)
-        await_send(2, s2a.at[t], t)
-
-    peers(drain_early)
+    await_all(send.at[0], others(r1a))
+    await_all(send.at[1], others(r1b, 8))
+    await_all(send.at[2], others(r2a))
 
     back = (8 * ((iota((64, 64), 1) % 16) // 2) + 2 * (iota((64, 64), 1) // 16) + iota((64, 64), 1) % 2
             == iota((64, 64), 0)).astype(F32).astype(BF)
@@ -282,13 +284,17 @@
 
     @pl.loop(0, 4)
     def _(step):
-        c = (me // 8 + jnp.where(step < 2, step, 5 - step)) % 4
-
-        @pl.loop(0, 8)
-        def _(h):
-            @pl.when(8 * c + h != me)
-            def _():
-                await_recv(3, r2b.at[pl.ds((8 * c + h) * 8, 8)], 8 * c + h)
+        c = lax.rem(lax.div(me, 8) + 6 + lax.div(step + 1, 2) * (1 - 2 * lax.rem(step, 2)), 4)
+
+        mine = c == lax.div(me, 8)
+
+        @pl.when(mine)
+        def _():
+            await_all(recv.at[8 + c], r2b.at[pl.ds(0, 56)])
+
+        @pl.when(jnp.logical_not(mine))
+        def _():
+            await_all(recv.at[8 + c], r2b.at[pl.ds(0, 64)])
 
         col = lambda base, h: pl.ds(pl.multiple_of((base + h) * 128, 128), 128)
         both = r2b[pl.ds(64 * c, 64)].astype(F32)
@@ -319,7 +325,8 @@
                 t12[8 * b + 4 + c, j] = dv[at:at + 16].astype(BF)
         store_branch(c).start()
         for b in range(8):
-            t = 4 * b + c
+            far = (b + 1) // 2 * (1 - 2 * (b % 2))
+            t = 4 * lax.rem(lax.div(me, NY) + 12 + far, NZ) + c
 
             @pl.when(t != me)
             def _():
@@ -331,27 +338,23 @@
     peers(lambda t: copy(6, g, rg.at[me], t).start())
     rg[me] = g[...]
 
-    peers(lambda t: await_recv(4, rt0.at[t], t))
+    await_all(recv.at[4], others(rt0))
     total = contract(m0[...], rt0[...].reshape(512, 128), 1, 0)
-
-    def drain_later(t):
-        await_send(3, s2b.at[pl.ds(t * 8, 8)], t)
-        await_send(4, t0.at[t], t)
-
-    peers(drain_later)
-    peers(lambda t: await_recv(5, rt12.at[t], t))
+    await_all(send.at[3], others(r2b, 8))
+    await_all(send.at[4], others(rt0))
+    await_all(recv.at[5], others(rt12))
     total += contract(m12[...], rt12[...].reshape(1024, 128), 1, 0)
     s4[...] = total.astype(BF).reshape(N, 16, 128)
     peers(lambda t: copy(7, s4.at[t], r4.at[me], t).start())
     r4[me] = s4[me]
 
-    peers(lambda t: await_recv(6, rg.at[t], t))
+    await_all(recv.at[6], others(rg))
     gd[...] = jnp.sum(rg[...], axis=0)
 
     def dp_copy(k):
         t = dp_peer(k)
         return pltpu.make_async_remote_copy(
-            src_ref=gd, dst_ref=rd.at[group], send_sem=dsend.at[t], recv_sem=drecv.at[group],
+            src_ref=gd, dst_ref=rd.at[group], send_sem=dsem.at[0], recv_sem=dsem.at[1],
             device_id={"dp": t}, device_id_type=MESH,
         )
 
@@ -361,7 +364,7 @@
 
     rd[group] = gd[...]
 
-    peers(lambda t: await_recv(7, r4.at[t], t))
+    await_all(recv.at[7], others(r4))
     for c in range(4):
         cols = slice(c * 128, (c + 1) * 128)
         x = pre_k[:, cols].astype(F32)
@@ -372,10 +375,7 @@
     stores[3].start()
     stores[4].start()
 
-    @pl.loop(1, n_dp)
-    def _(k):
-        t = dp_peer(k)
-        pltpu.make_async_copy(rd.at[t], rd.at[t], drecv.at[t]).wait()
+    await_all(dsem.at[1], rd.at[pl.ds(0, n_dp - 1)])
 
     sums = jnp.sum(rd[...], axis=0)
     out_qg[...] = sums[0:1]
@@ -383,18 +383,10 @@
     stores[5].start()
     stores[6].start()
 
-    def drain(t):
-        await_send(5, t12.at[t], t)
-        await_send(6, g, t)
-        await_send(7, s4.at[t], t)
-
-    peers(drain)
-
-    @pl.loop(1, n_dp)
-    def _(k):
-        t = dp_peer(k)
-        pltpu.make_async_copy(gd, gd, dsend.at[t]).wait()
-
+    await_all(send.at[5], others(rt12))
+    await_all(send.at[6], others(rg))
+    await_all(send.at[7], others(r4))
+    await_all(dsem.at[0], rd.at[pl.ds(0, n_dp - 1)])
     for each in stores:
         each.wait()
 
@@ -487,10 +479,9 @@
             pltpu.VMEM((64, 512), F32),
             pltpu.VMEM((64, 512), F32),
             pltpu.VMEM((64, 512), F32),
-            pltpu.SemaphoreType.DMA((8, N)),
-            pltpu.SemaphoreType.DMA((8, N)),
-            pltpu.SemaphoreType.DMA((n_dp,)),
-            pltpu.SemaphoreType.DMA((n_dp,)),
+            pltpu.SemaphoreType.DMA((8,)),
+            pltpu.SemaphoreType.DMA((12,)),
+            pltpu.SemaphoreType.DMA((2,)),
         ],
         compiler_params=pltpu.CompilerParams(
             collective_id=0, has_side_effects=True, vmem_limit_bytes=60 * 1024 * 1024

time: 105 us -> 95.5 us (0.910); the launches traced: 103 us -> 95.4 us
  Pallas kernels: 103 us -> 94.7 us
    pallas_call x1, Pallas kernels: 101 us -> 92.6 us  [body(): pl.pallas_call(kernel, out_shape=(jax.ShapeDtypeStruct((128, 4096), BF),...]
where the time goes in v3:
time: 95.5 us; the launch traced here: 95.4 us
  Pallas kernels  94.7 us (99%)
    pallas_call x1, Pallas kernels, body(): pl.pallas_call(kernel, out_shape=(jax.ShapeDtypeStruct((128, 4096), BF),...  92.6 us
    pallas_call x1, Pallas kernels, body(): pl.pallas_call(write_out, out_shape=tuple((jax.ShapeDtypeStruct(x.shape,...  2.14 us

profile of v3, /device:TPU:1, one launch (start us, length us, event | category | flops | bytes accessed | tf_op | source)
XLA Modules:
  0.0 95.4 jit_solution(11019041165534730916)
XLA Ops:
  0.6 92.6 %shard_map.173 = (bf16[128,4096]{1,0:T(8,128)(2,1)}, bf16[128,512]{1,0:T(8,128)(2,1)}, bf16[128,512]{1,0:T(8,128)(2,1)}, f32[1,128]{1,0:T(1,128)}, f32[1,128]{1,0:T(1,128)}) custom-call(bf16[64,4096]{1,0:T(8,128)(2,1)} %refs_0_.1, bf16[64,512]{1,0:T(8,128)(2,1)} %refs_1_.1, bf16[64,512]{1,0:T(8,128)(2,1)} %refs_2_.1, bf16[64,4096]{1,0:T(8,128)(2,1)} %refs_3_.1, ...), custom_call_target="tpu_custom_call" | custom-call | tf_op jit(solution)/shard_map/pallas_call | solution.py:420
  93.3 2.1 %shard_map.174 = (bf16[128,4096]{1,0:T(8,128)(2,1)}, bf16[128,512]{1,0:T(8,128)(2,1)}, bf16[128,512]{1,0:T(8,128)(2,1)}, f32[1,128]{1,0:T(1,128)}, f32[1,128]{1,0:T(1,128)}) custom-call(bf16[128,4096]{1,0:T(8,128)(2,1)} %get-tuple-element.15.refs_0_, bf16[128,512]{1,0:T(8,128)(2,1)} %get-tuple-element.16.refs_1_, ...), custom_call_target="tpu_custom_call" | custom-call | tf_op jit(solution)/shard_map/pallas_call | solution.py:495

commit v4 on v3

--- a/solution.py
+++ b/solution.py
@@ -10,6 +10,7 @@
 EPSILON = 1e-06
 NZ, NY = 8, 4
 N = NZ * NY
+NEAR = N // 2
 BF = jnp.bfloat16
 F32 = jnp.float32
 MESH = pl.DeviceIdType.MESH
@@ -57,7 +58,7 @@
 
 def compute(
     ins, outs, staged, held, small, table, loaded, indexed,
-    stored, kv, r1a, s1b, r1b, s2a, r2a, s2b, r2b, t0, rt0, t12, rt12, s4, r4,
+    stored, pkv, rkv, s1a, r1a, s1b, r1b, s2a, r2a, s2b, r2b, t0, rt0, t12, rt12, s4, r4,
     g, rg, gd, rd, m0, m12, dkp, dvp, causal, send, recv, dsem,
 ):
     pre_q, pre_k, pre_v, pre_c, gen_q, gen_k, gen_v, gen_c, qg, kg, dest_row, pp_row, bp_row, rew_row = held
@@ -94,6 +95,13 @@
     def others(ref, size=1):
         return ref.at[pl.ds(0, (N - 1) * size)]
 
+    def near_others(ref):
+        return ref.at[pl.ds(0, NEAR - 1)]
+
+    def near(j, dy, sign):
+        dz = 2 - 4 * lax.rem(dy, 2) if j == 0 else (0, 1, -1, 0)[j]
+        return lax.rem(lax.div(me, NY) + NZ + sign * dz, NZ) * NY + lax.rem(me + NY + sign * dy, NY)
+
     def store(i, output, rows):
         return pltpu.make_async_copy(staged[output].at[rows], outs[output].at[rows], stored.at[i])
 
@@ -129,27 +137,32 @@
 
     for c in range(4):
         x = pre_k[:, c * 128:(c + 1) * 128].astype(F32)
-        kv[0, :, c * 128:(c + 1) * 128] = (x * inverse_norm(x) * kgain).astype(BF)
-    kv[0, :, 512:] = pre_v[...]
+        pkv[0, :, c * 128:(c + 1) * 128] = (x * inverse_norm(x) * kgain).astype(BF)
+    pkv[1] = pre_v[...]
     rows = iota((64, 64), 0)
     spread = (8 * ((rows % 16) // 2) + 2 * (rows // 16) + rows % 2 == iota((64, 64), 1)).astype(F32).astype(BF)
-    kv[1, :, :512] = contract(spread, gen_k[...], 1, 0).astype(BF)
-    kv[1, :, 512:] = contract(spread, gen_v[...], 1, 0).astype(BF)
+    rkv[:, :512] = contract(spread, gen_k[...], 1, 0).astype(BF)
+    rkv[:, 512:] = contract(spread, gen_v[...], 1, 0).astype(BF)
 
     for i in (4, 7):
         fetch[i].wait()
     pl.semaphore_wait(barrier, N - 1 + n_dp - 1)
 
-    def fragment(t):
-        rb = pl.multiple_of((t // 8) * 16, 16)
-        cb = pl.multiple_of((t % 8) * 128, 128)
-        return kv.at[:, pl.ds(rb, 16), pl.ds(cb, 128)]
+    def fill_1a(t):
+        rb = pl.multiple_of(lax.rem(lax.div(t, 4), 4) * 16, 16)
+        cb = pl.multiple_of(lax.rem(t, 4) * 128, 128)
+        s1a[t, 0:2] = pkv[:, pl.ds(rb, 16), pl.ds(cb, 128)]
+        rp = pl.multiple_of(lax.rem(t, 4) * 16, 16)
+        cr = pl.multiple_of((lax.div(t, 8) + 4 * lax.rem(lax.div(t, 4), 2)) * 128, 128)
+        s1a[t, 2] = rkv[pl.ds(rp, 16), pl.ds(cr, 128)]
 
     def send_1a(t):
-        copy(0, fragment(t), r1a.at[me], t).start()
+        fill_1a(t)
+        copy(0, s1a.at[t], r1a.at[me], t).start()
 
     peers(send_1a)
-    r1a[me] = fragment(me)[...]
+    fill_1a(me)
+    r1a[me] = s1a[me]
 
     def slab(t):
         cols = pl.ds(pl.multiple_of(t * 128, 128), 128)
@@ -180,16 +193,21 @@
     bp = jnp.broadcast_to(bp_row[...].astype(F32), (8, N))
     pick = (bp_row[...] == iota((N, N), 0)).astype(F32).astype(BF)
     upper = contract(pp.astype(BF), pick, 1, 0)
-    spread0 = (iota((N, 512), 0) == iota((N, 512), 1) // 16).astype(F32).astype(BF)
-    row0 = (iota((8, 512), 1) % 16).astype(F32)
-    spread1 = (iota((N, 1024), 0) == iota((N, 1024), 1) // 32).astype(F32).astype(BF)
-    lane1 = iota((8, 1024), 1)
-    id0 = contract(pp.astype(BF), spread0, 1, 0) * 16.0 + row0
+    def clients(lane, each):
+        k = lane // each
+        j, dy = k // NY, k % NY
+        dz = jnp.where(j == 0, 2 - 4 * (dy % 2), jnp.where(j == 1, 1, jnp.where(j == 2, -1, 0)))
+        at = (lax.div(me, NY) + NZ + dz) % NZ * NY + (me + dy) % NY
+        return (iota(lane.shape, 0) == at).astype(F32).astype(BF)
+
+    lane0, lane1 = iota((N, 256), 1), iota((N, 512), 1)
+    id0 = contract(pp.astype(BF), clients(lane0, 16), 1, 0) * 16.0 + (lane0 % 16).astype(F32)[:8]
+    spread1 = clients(lane1, 32)
     parent1 = contract(bp.astype(BF), spread1, 1, 0)
     upper1 = contract(upper.astype(BF), spread1, 1, 0)
-    id1 = jnp.where((lane1 // 16) % 2 == 0, parent1, upper1) * 16.0 + (lane1 % 16).astype(F32)
-    m0[...] = (iota((512, 512), 0).astype(F32) == id0[:1]).astype(F32).astype(BF)
-    m12[...] = (iota((512, 1024), 0).astype(F32) == id1[:1]).astype(F32).astype(BF)
+    id1 = jnp.where(((lane1 // 16) % 2 == 0)[:8], parent1, upper1) * 16.0 + (lane1 % 16).astype(F32)[:8]
+    m0[...] = (iota((512, 256), 0).astype(F32) == id0[:1]).astype(F32).astype(BF)
+    m12[...] = (iota((512, 512), 0).astype(F32) == id1[:1]).astype(F32).astype(BF)
     dest = jnp.broadcast_to(dest_row[...].astype(F32), (8, 256)).astype(BF)
     spread2 = (iota((256, 512), 0) == iota((256, 512), 1) // 2).astype(F32).astype(BF)
     id2 = contract(dest, spread2, 1, 0) * 2.0 + (iota((8, 512), 1) % 2).astype(F32)
@@ -209,40 +227,41 @@
     adv = ((rew_s[0, me].astype(F32) - center) / jnp.maximum(jnp.sqrt(var), 1.0))[:1]
 
     await_all(recv.at[0], others(r1a))
-    s2a[:, 3] = contract(order, r1a[:, 1].reshape(512, 128), 1, 0).astype(BF).reshape(N, 16, 128)
-
-    def fill_2a(t):
-        parent = bp_s[0, t]
-        s2a[t, 0] = r1a[jnp.maximum(pp_s[0, t], 0), 0]
-        s2a[t, 1] = r1a[parent, 0]
-        s2a[t, 2] = r1a[jnp.maximum(pp_s[0, parent], 0), 0]
-
-    def send_2a(t):
-        fill_2a(t)
-        copy(2, s2a.at[t], r2a.at[me], t).start()
-
-    peers(send_2a)
-    fill_2a(me)
-    r2a[me] = s2a[me]
+    for j in range(4):
+        for dy in (2, 1, 3, 0):
+            t = near(j, dy, 1)
+            k = 4 * j + dy
+            parent = bp_s[0, t]
+            s2a[k, 0] = r1a[jnp.maximum(pp_s[0, t], 0), 0:2]
+            s2a[k, 1] = r1a[parent, 0:2]
+            s2a[k, 2] = r1a[jnp.maximum(pp_s[0, parent], 0), 0:2]
+            if k != 12:
+                copy(2, s2a.at[k], r2a.at[lax.rem(me, NEAR)], t).start()
+    r2a[lax.rem(me, NEAR)] = s2a[12]
+    s2b[:, 8] = contract(order, r1a[:, 2].reshape(512, 128), 1, 0).astype(BF).reshape(N, 16, 128)
 
     lookup.wait()
     await_all(recv.at[1], others(r1b, 8))
 
     def send_2b(t):
         for p in range(8):
-            s2b[t * 8 + p] = r1b[inv_s[0, t * 8 + p]]
-        copy(3, s2b.at[pl.ds(t * 8, 8)], r2b.at[pl.ds(me * 8, 8)], t).start()
+            s2b[t, p] = r1b[inv_s[0, t * 8 + p]]
+        copy(3, s2b.at[t], r2b.at[me], t).start()
 
     peers(send_2b)
     for p in range(8):
-        r2b[me * 8 + p] = r1b[inv_s[0, me * 8 + p]]
-
-    def tiles(ref, at, c):
-        return jnp.concatenate([ref[8 * b + c] if at is None else ref[8 * b + c, at] for b in range(4)], axis=0)
+        r2b[me, p] = r1b[inv_s[0, me * 8 + p]]
+    r2b[me, 8] = s2b[me, 8]
+
+    def above_rows(slot, which, c):
+        return jnp.concatenate([r2a[4 * b + c, slot, which] for b in range(4)], axis=0)
+
+    def own_rows(first):
+        return jnp.concatenate([r2b[first + b, 8] for b in range(4)], axis=0)
 
     for i in (0, 3):
         fetch[i].wait()
-    await_all(recv.at[2], others(r2a))
+    await_all(recv.at[2], near_others(r2a))
     g[...] = jnp.zeros((8, 128), F32)
     above = (my_above >= 0).astype(F32)
 
@@ -251,10 +270,10 @@
         col = lambda base, h: pl.ds(pl.multiple_of((base + h) * 128, 128), 128)
         q = jnp.concatenate([pre_q[:, col(8 * c, h)] for h in range(8)], axis=0).astype(F32)
         cot = jnp.concatenate([pre_c[:, col(8 * c, h)] for h in range(8)], axis=0)
-        own_k = kv[0, :, col(c, 0)]
-        far_k = tiles(r2a, 0, c)
+        own_k = pkv[0, :, col(c, 0)]
+        far_k = above_rows(0, 0, c)
         keys = jnp.concatenate([own_k, far_k], axis=0)
-        vals = jnp.concatenate([kv[0, :, col(c, 4)], tiles(r2a, 0, 4 + c)], axis=0)
+        vals = jnp.concatenate([pkv[1, :, col(c, 0)], above_rows(0, 1, c)], axis=0)
         mask = jnp.concatenate([causal[...], jnp.full((64, 512), 1.0, F32) * above], axis=0)
         dq, dk, dv, q_term = attend(q, cot, qgain, keys, vals, mask)
         for h in range(8):
@@ -267,16 +286,20 @@
         g[0:1] += q_term
         g[1:2] += k_term
         for b in range(4):
-            t0[8 * b + c] = dk[64 + 16 * b:80 + 16 * b].astype(BF)
-            t0[8 * b + 4 + c] = dv[64 + 16 * b:80 + 16 * b].astype(BF)
+            t0[4 * b + c, 0] = dk[64 + 16 * b:80 + 16 * b].astype(BF)
+            t0[4 * b + c, 1] = dv[64 + 16 * b:80 + 16 * b].astype(BF)
 
     stores[0].start()
-    peers(lambda t: copy(4, t0.at[t], rt0.at[me], t).start())
-    rt0[me] = t0[me]
+    for j in range(4):
+        for dy in (2, 1, 3, 0):
+            t = near(j, dy, -1)
+            if 4 * j + dy != 12:
+                copy(4, t0.at[lax.rem(t, NEAR)], rt0.at[4 * j + dy], t).start()
+    rt0[12] = t0[lax.rem(me, NEAR)]
 
     await_all(send.at[0], others(r1a))
     await_all(send.at[1], others(r1b, 8))
-    await_all(send.at[2], others(r2a))
+    await_all(send.at[2], near_others(r2a))
 
     back = (8 * ((iota((64, 64), 1) % 16) // 2) + 2 * (iota((64, 64), 1) // 16) + iota((64, 64), 1) % 2
             == iota((64, 64), 0)).astype(F32).astype(BF)
@@ -290,22 +313,22 @@
 
         @pl.when(mine)
         def _():
-            await_all(recv.at[8 + c], r2b.at[pl.ds(0, 56)])
+            await_all(recv.at[8 + c], r2b.at[pl.ds(0, 7)])
 
         @pl.when(jnp.logical_not(mine))
         def _():
-            await_all(recv.at[8 + c], r2b.at[pl.ds(0, 64)])
+            await_all(recv.at[8 + c], r2b.at[pl.ds(0, 8)])
 
         col = lambda base, h: pl.ds(pl.multiple_of((base + h) * 128, 128), 128)
-        both = r2b[pl.ds(64 * c, 64)].astype(F32)
+        both = r2b[pl.ds(8 * c, 8), 0:8].reshape(64, 16, 128).astype(F32)
         q = both[:, :8].reshape(512, 128)
         cot = (both[:, 8:].reshape(512, 128) * adv).astype(BF)
-        x = contract(back, tiles(r2a, 3, c), 1, 0)
+        x = contract(back, own_rows(8 * c), 1, 0)
         r = inverse_norm(x)
-        far_k = jnp.concatenate([tiles(r2a, 1, c), tiles(r2a, 2, c)], axis=0)
+        far_k = jnp.concatenate([above_rows(1, 0, c), above_rows(2, 0, c)], axis=0)
         keys = jnp.concatenate([(x * r * kgain).astype(BF), far_k], axis=0)
         vals = jnp.concatenate(
-            [contract(back, tiles(r2a, 3, 4 + c), 1, 0).astype(BF), tiles(r2a, 1, 4 + c), tiles(r2a, 2, 4 + c)], axis=0
+            [contract(back, own_rows(8 * c + 4), 1, 0).astype(BF), above_rows(1, 1, c), above_rows(2, 1, c)], axis=0
         )
         ones = jnp.full((64, 512), 1.0, F32)
         mask = jnp.concatenate([causal[...], ones, ones * upper_ok], axis=0)
@@ -321,30 +344,34 @@
         for b in range(4):
             for j in range(2):
                 at = 64 + 64 * j + 16 * b
-                t12[8 * b + c, j] = dk[at:at + 16].astype(BF)
-                t12[8 * b + 4 + c, j] = dv[at:at + 16].astype(BF)
+                t12[4 * b + c, j, 0] = dk[at:at + 16].astype(BF)
+                t12[4 * b + c, j, 1] = dv[at:at + 16].astype(BF)
         store_branch(c).start()
-        for b in range(8):
-            far = (b + 1) // 2 * (1 - 2 * (b % 2))
-            t = 4 * lax.rem(lax.div(me, NY) + 12 + far, NZ) + c
+        dy = lax.rem(me + 4 - c, NY)
+        for j in range(4):
+            t = near(j, dy, -1)
 
             @pl.when(t != me)
             def _():
-                copy(5, t12.at[t], rt12.at[me], t).start()
-
-    rt12[me] = t12[me]
+                copy(5, t12.at[lax.rem(t, NEAR)], rt12.at[4 * j + dy], t).start()
+
+    rt12[12] = t12[lax.rem(me, NEAR)]
     stores[1].start()
     stores[2].start()
     peers(lambda t: copy(6, g, rg.at[me], t).start())
     rg[me] = g[...]
 
-    await_all(recv.at[4], others(rt0))
-    total = contract(m0[...], rt0[...].reshape(512, 128), 1, 0)
-    await_all(send.at[3], others(r2b, 8))
-    await_all(send.at[4], others(rt0))
-    await_all(recv.at[5], others(rt12))
-    total += contract(m12[...], rt12[...].reshape(1024, 128), 1, 0)
-    s4[...] = total.astype(BF).reshape(N, 16, 128)
+    def columns(first, second, rows):
+        return jnp.concatenate([first.reshape(rows, 128), second.reshape(rows, 128)], axis=1)
+
+    await_all(recv.at[4], near_others(rt0))
+    total = contract(m0[...], columns(rt0[:, 0], rt0[:, 1], 256), 1, 0)
+    await_all(send.at[3], others(r2b))
+    await_all(send.at[4], near_others(rt0))
+    await_all(recv.at[5], near_others(rt12))
+    total += contract(m12[...], columns(rt12[:, :, 0], rt12[:, :, 1], 512), 1, 0)
+    s4[:, 0] = total[:, :128].astype(BF).reshape(N, 16, 128)
+    s4[:, 1] = total[:, 128:].astype(BF).reshape(N, 16, 128)
     peers(lambda t: copy(7, s4.at[t], r4.at[me], t).start())
     r4[me] = s4[me]
 
@@ -365,12 +392,16 @@
     rd[group] = gd[...]
 
     await_all(recv.at[7], others(r4))
+    def far_rows(which, c):
+        pairs = [r4[4 * b + c, which].astype(F32) + r4[NEAR + 4 * b + c, which].astype(F32) for b in range(4)]
+        return jnp.concatenate(pairs, axis=0)
+
     for c in range(4):
         cols = slice(c * 128, (c + 1) * 128)
         x = pre_k[:, cols].astype(F32)
-        dk = dkp[:, cols] + tiles(r4, None, c).astype(F32)
+        dk = dkp[:, cols] + far_rows(0, c)
         out_k[0:64, cols] = norm_back(x, inverse_norm(x), kgain, dk).astype(BF)
-        out_v[0:64, cols] = (dvp[:, cols] + tiles(r4, None, 4 + c).astype(F32)).astype(BF)
+        out_v[0:64, cols] = (dvp[:, cols] + far_rows(1, c)).astype(BF)
 
     stores[3].start()
     stores[4].start()
@@ -383,7 +414,7 @@
     stores[5].start()
     stores[6].start()
 
-    await_all(send.at[5], others(rt12))
+    await_all(send.at[5], near_others(rt12))
     await_all(send.at[6], others(rg))
     await_all(send.at[7], others(r4))
     await_all(dsem.at[0], rd.at[pl.ds(0, n_dp - 1)])
@@ -456,26 +487,28 @@
             pltpu.VMEM((1, 128), F32),
             pltpu.VMEM((1, 128), F32),
             pltpu.SemaphoreType.DMA((11,)),
-            pltpu.VMEM((2, 64, 1024), BF),
-            pltpu.VMEM((N, 2, 16, 128), BF),
+            pltpu.VMEM((2, 64, 512), BF),
+            pltpu.VMEM((64, 1024), BF),
+            pltpu.VMEM((N, 3, 16, 128), BF),
+            pltpu.VMEM((N, 3, 16, 128), BF),
             pltpu.VMEM((256, 16, 128), BF),
             pltpu.VMEM((256, 16, 128), BF),
-            pltpu.VMEM((N, 4, 16, 128), BF),
-            pltpu.VMEM((N, 4, 16, 128), BF),
-            pltpu.VMEM((256, 16, 128), BF),
-            pltpu.VMEM((256, 16, 128), BF),
-            pltpu.VMEM((N, 16, 128), BF),
-            pltpu.VMEM((N, 16, 128), BF),
+            pltpu.VMEM((NEAR, 3, 2, 16, 128), BF),
+            pltpu.VMEM((NEAR, 3, 2, 16, 128), BF),
+            pltpu.VMEM((N, 9, 16, 128), BF),
+            pltpu.VMEM((N, 9, 16, 128), BF),
+            pltpu.VMEM((NEAR, 2, 16, 128), BF),
+            pltpu.VMEM((NEAR, 2, 16, 128), BF),
+            pltpu.VMEM((NEAR, 2, 2, 16, 128), BF),
+            pltpu.VMEM((NEAR, 2, 2, 16, 128), BF),
             pltpu.VMEM((N, 2, 16, 128), BF),
             pltpu.VMEM((N, 2, 16, 128), BF),
-            pltpu.VMEM((N, 16, 128), BF),
-            pltpu.VMEM((N, 16, 128), BF),
             pltpu.VMEM((8, 128), F32),
             pltpu.VMEM((N, 8, 128), F32),
             pltpu.VMEM((8, 128), F32),
             pltpu.VMEM((n_dp, 8, 128), F32),
+            pltpu.VMEM((512, 256), BF),
             pltpu.VMEM((512, 512), BF),
-            pltpu.VMEM((512, 1024), BF),
             pltpu.VMEM((64, 512), F32),
             pltpu.VMEM((64, 512), F32),
             pltpu.VMEM((64, 512), F32),

time: 95.5 us -> 92.5 us (0.969)
  Pallas kernels: 94.7 us -> 91.1 us
    pallas_call x1, Pallas kernels: 92.6 us -> 89 us  [body(): pl.pallas_call(kernel, out_shape=(jax.ShapeDtypeStruct((128, 4096), BF),...]
where the time goes in v4:
time: 92.5 us; the launch traced here: 91.8 us
  Pallas kernels  91.1 us (98%)
    pallas_call x1, Pallas kernels, body(): pl.pallas_call(kernel, out_shape=(jax.ShapeDtypeStruct((128, 4096), BF),...  89 us
    pallas_call x1, Pallas kernels, body(): pl.pallas_call(write_out, out_shape=tuple((jax.ShapeDtypeStruct(x.shape,...  2.14 us

profile of v4, /device:TPU:1, one launch (start us, length us, event | category | flops | bytes accessed | tf_op | source)
XLA Modules:
  0.0 91.8 jit_solution(2668801801151528408)
XLA Ops:
  0.6 89.0 %shard_map.173 = (bf16[128,4096]{1,0:T(8,128)(2,1)}, bf16[128,512]{1,0:T(8,128)(2,1)}, bf16[128,512]{1,0:T(8,128)(2,1)}, f32[1,128]{1,0:T(1,128)}, f32[1,128]{1,0:T(1,128)}) custom-call(bf16[64,4096]{1,0:T(8,128)(2,1)} %refs_0_.1, bf16[64,512]{1,0:T(8,128)(2,1)} %refs_1_.1, bf16[64,512]{1,0:T(8,128)(2,1)} %refs_2_.1, bf16[64,4096]{1,0:T(8,128)(2,1)} %refs_3_.1, ...), custom_call_target="tpu_custom_call" | custom-call | tf_op jit(solution)/shard_map/pallas_call | solution.py:451
  89.6 2.1 %shard_map.174 = (bf16[128,4096]{1,0:T(8,128)(2,1)}, bf16[128,512]{1,0:T(8,128)(2,1)}, bf16[128,512]{1,0:T(8,128)(2,1)}, f32[1,128]{1,0:T(1,128)}, f32[1,128]{1,0:T(1,128)}) custom-call(bf16[128,4096]{1,0:T(8,128)(2,1)} %get-tuple-element.15.refs_0_, bf16[128,512]{1,0:T(8,128)(2,1)} %get-tuple-element.16.refs_1_, ...), custom_call_target="tpu_custom_call" | custom-call | tf_op jit(solution)/shard_map/pallas_call | solution.py:528

commit v5 on v4

--- a/solution.py
+++ b/solution.py
@@ -35,19 +35,18 @@
     return r * scaled - x * (r * r * r) * inner
 
 
-def attend(q, cot, gain, keys, vals, mask):
-    r = inverse_norm(q)
-    qn = (q * r * gain).astype(BF)
+def attend_keys(q, cot, gain, keys, vals, mask):
+    qn = (q * inverse_norm(q) * gain).astype(BF)
     weights = jnp.exp(contract(keys, qn, 1, 1) * SCALE) * mask
     probs = weights * (1.0 / jnp.sum(weights, axis=0, keepdims=True))
     dprob = contract(vals, cot, 1, 1)
     inner = jnp.sum(probs * dprob, axis=0, keepdims=True)
     dscore = (probs * (dprob - inner) * SCALE).astype(BF)
-    dq = contract(dscore, keys, 0, 0)
-    dk = contract(dscore, qn, 1, 0)
-    dv = contract(probs.astype(BF), cot, 1, 0)
-    gain_term = jnp.sum(dq * q * r, axis=0, keepdims=True)
-    return norm_back(q, r, gain, dq), dk, dv, gain_term
+    return dscore, contract(dscore, qn, 1, 0), contract(probs.astype(BF), cot, 1, 0)
+
+
+def attend_queries(q, gain, keys, dscore):
+    return norm_back(q, inverse_norm(q), gain, contract(dscore, keys, 0, 0))
 
 
 def kernel(*refs):
@@ -58,7 +57,7 @@
 
 def compute(
     ins, outs, staged, held, small, table, loaded, indexed,
-    stored, pkv, rkv, s1a, r1a, s1b, r1b, s2a, r2a, s2b, r2b, t0, rt0, t12, rt12, s4, r4,
+    stored, dscores, allkeys, branch_x, dkb, pkv, rkv, s1a, r1a, s1b, r1b, s2a, r2a, s2b, r2b, t0, rt0, t12, rt12, s4, r4,
     g, rg, gd, rd, m0, m12, dkp, dvp, causal, send, recv, dsem,
 ):
     pre_q, pre_k, pre_v, pre_c, gen_q, gen_k, gen_v, gen_c, qg, kg, dest_row, pp_row, bp_row, rew_row = held
@@ -262,7 +261,7 @@
     for i in (0, 3):
         fetch[i].wait()
     await_all(recv.at[2], near_others(r2a))
-    g[...] = jnp.zeros((8, 128), F32)
+    g[...] = jnp.zeros((1, 128), F32)
     above = (my_above >= 0).astype(F32)
 
     @pl.loop(0, 4)
@@ -275,16 +274,13 @@
         keys = jnp.concatenate([own_k, far_k], axis=0)
         vals = jnp.concatenate([pkv[1, :, col(c, 0)], above_rows(0, 1, c)], axis=0)
         mask = jnp.concatenate([causal[...], jnp.full((64, 512), 1.0, F32) * above], axis=0)
-        dq, dk, dv, q_term = attend(q, cot, qgain, keys, vals, mask)
+        dscore, dk, dv = attend_keys(q, cot, qgain, keys, vals, mask)
+        dq = attend_queries(q, qgain, keys, dscore)
         for h in range(8):
             out_q[0:64, col(8 * c, h)] = dq[h * 64:(h + 1) * 64].astype(BF)
         dkp[:, col(c, 0)] = dk[:64]
         dvp[:, col(c, 0)] = dv[:64]
-        x = pre_k[:, col(c, 0)].astype(F32)
-        k_term = jnp.sum(dk[:64] * x * inverse_norm(x), axis=0, keepdims=True)
-        k_term += jnp.sum(dk[64:] * far_k.astype(F32), axis=0, keepdims=True) / kgain
-        g[0:1] += q_term
-        g[1:2] += k_term
+        g[...] += jnp.sum(dk * keys.astype(F32), axis=0, keepdims=True)
         for b in range(4):
             t0[4 * b + c, 0] = dk[64 + 16 * b:80 + 16 * b].astype(BF)
             t0[4 * b + c, 1] = dv[64 + 16 * b:80 + 16 * b].astype(BF)
@@ -332,21 +328,12 @@
         )
         ones = jnp.full((64, 512), 1.0, F32)
         mask = jnp.concatenate([causal[...], ones, ones * upper_ok], axis=0)
-        dq, dk, dv, q_term = attend(q, cot, qgain, keys, vals, mask)
-        for h in range(8):
-            out_q[64:128, col(8 * c, h)] = dq[h * 64:(h + 1) * 64].astype(BF)
-        out_k[64:128, col(c, 0)] = norm_back(x, r, kgain, dk[:64]).astype(BF)
-        out_v[64:128, col(c, 0)] = dv[:64].astype(BF)
-        k_term = jnp.sum(dk[:64] * x * r, axis=0, keepdims=True)
-        k_term += jnp.sum(dk[64:] * far_k.astype(F32), axis=0, keepdims=True) / kgain
-        g[0:1] += q_term
-        g[1:2] += k_term
+        dscore, dk, dv = attend_keys(q, cot, qgain, keys, vals, mask)
         for b in range(4):
             for j in range(2):
                 at = 64 + 64 * j + 16 * b
                 t12[4 * b + c, j, 0] = dk[at:at + 16].astype(BF)
                 t12[4 * b + c, j, 1] = dv[at:at + 16].astype(BF)
-        store_branch(c).start()
         dy = lax.rem(me + 4 - c, NY)
         for j in range(4):
             t = near(j, dy, -1)
@@ -355,11 +342,31 @@
             def _():
                 copy(5, t12.at[lax.rem(t, NEAR)], rt12.at[4 * j + dy], t).start()
 
+        out_v[64:128, col(c, 0)] = dv[:64].astype(BF)
+        dscores[c] = dscore
+        allkeys[c] = keys
+        branch_x[:, col(c, 0)] = x
+        dkb[:, col(c, 0)] = dk[:64]
+        g[...] += jnp.sum(dk * keys.astype(F32), axis=0, keepdims=True)
+
     rt12[12] = t12[lax.rem(me, NEAR)]
+
+    peers(lambda t: copy(6, g, rg.at[me], t).start())
+    rg[me] = g[...]
+
+    @pl.loop(0, 4)
+    def _(c):
+        col = lambda base, h: pl.ds(pl.multiple_of((base + h) * 128, 128), 128)
+        q = r2b[pl.ds(8 * c, 8), 0:8].reshape(64, 16, 128).astype(F32)[:, :8].reshape(512, 128)
+        dq = attend_queries(q, qgain, allkeys[c], dscores[c])
+        for h in range(8):
+            out_q[64:128, col(8 * c, h)] = dq[h * 64:(h + 1) * 64].astype(BF)
+        store_branch(c).start()
+        x, dk = branch_x[:, col(c, 0)], dkb[:, col(c, 0)]
+        out_k[64:128, col(c, 0)] = norm_back(x, inverse_norm(x), kgain, dk).astype(BF)
+
     stores[1].start()
     stores[2].start()
-    peers(lambda t: copy(6, g, rg.at[me], t).start())
-    rg[me] = g[...]
 
     def columns(first, second, rows):
         return jnp.concatenate([first.reshape(rows, 128), second.reshape(rows, 128)], axis=1)
@@ -372,7 +379,13 @@
     total += contract(m12[...], columns(rt12[:, :, 0], rt12[:, :, 1], 512), 1, 0)
     s4[:, 0] = total[:, :128].astype(BF).reshape(N, 16, 128)
     s4[:, 1] = total[:, 128:].astype(BF).reshape(N, 16, 128)
-    peers(lambda t: copy(7, s4.at[t], r4.at[me], t).start())
+
+    @pl.loop(0, N)
+    def _(t):
+        @pl.when(t != me)
+        def _():
+            copy(7, s4.at[t], r4.at[me], t).start()
+
     r4[me] = s4[me]
 
     await_all(recv.at[6], others(rg))
@@ -409,8 +422,8 @@
     await_all(dsem.at[1], rd.at[pl.ds(0, n_dp - 1)])
 
     sums = jnp.sum(rd[...], axis=0)
-    out_qg[...] = sums[0:1]
-    out_kg[...] = sums[1:2]
+    out_qg[...] = sums / qgain
+    out_kg[...] = sums / kgain
     stores[5].start()
     stores[6].start()
 
@@ -487,6 +500,10 @@
             pltpu.VMEM((1, 128), F32),
             pltpu.VMEM((1, 128), F32),
             pltpu.SemaphoreType.DMA((11,)),
+            pltpu.VMEM((4, 192, 512), BF),
+            pltpu.VMEM((4, 192, 128), BF),
+            pltpu.VMEM((64, 512), F32),
+            pltpu.VMEM((64, 512), F32),
             pltpu.VMEM((2, 64, 512), BF),
             pltpu.VMEM((64, 1024), BF),
             pltpu.VMEM((N, 3, 16, 128), BF),
@@ -503,10 +520,10 @@
             pltpu.VMEM((NEAR, 2, 2, 16, 128), BF),
             pltpu.VMEM((N, 2, 16, 128), BF),
             pltpu.VMEM((N, 2, 16, 128), BF),
-            pltpu.VMEM((8, 128), F32),
-            pltpu.VMEM((N, 8, 128), F32),
-            pltpu.VMEM((8, 128), F32),
-            pltpu.VMEM((n_dp, 8, 128), F32),
+            pltpu.VMEM((1, 128), F32),
+            pltpu.VMEM((N, 1, 128), F32),
+            pltpu.VMEM((1, 128), F32),
+            pltpu.VMEM((n_dp, 1, 128), F32),
             pltpu.VMEM((512, 256), BF),
             pltpu.VMEM((512, 512), BF),
             pltpu.VMEM((64, 512), F32),

time: 92.5 us -> 91.1 us (0.985)
  Pallas kernels: 91.1 us -> 89.9 us
    pallas_call x1, Pallas kernels: 89 us -> 87.7 us  [body(): pl.pallas_call(kernel, out_shape=(jax.ShapeDtypeStruct((128, 4096), BF),...]
where the time goes in v5:
time: 91.1 us; the launch traced here: 90.5 us
  Pallas kernels  89.9 us (99%)
    pallas_call x1, Pallas kernels, body(): pl.pallas_call(kernel, out_shape=(jax.ShapeDtypeStruct((128, 4096), BF),...  87.7 us
    pallas_call x1, Pallas kernels, body(): pl.pallas_call(write_out, out_shape=tuple((jax.ShapeDtypeStruct(x.shape,...  2.14 us

profile of v5, /device:TPU:1, one launch (start us, length us, event | category | flops | bytes accessed | tf_op | source)
XLA Modules:
  0.0 90.5 jit_solution(8353256062723865869)
XLA Ops:
  0.6 87.7 %shard_map.173 = (bf16[128,4096]{1,0:T(8,128)(2,1)}, bf16[128,512]{1,0:T(8,128)(2,1)}, bf16[128,512]{1,0:T(8,128)(2,1)}, f32[1,128]{1,0:T(1,128)}, f32[1,128]{1,0:T(1,128)}) custom-call(bf16[64,4096]{1,0:T(8,128)(2,1)} %refs_0_.1, bf16[64,512]{1,0:T(8,128)(2,1)} %refs_1_.1, bf16[64,512]{1,0:T(8,128)(2,1)} %refs_2_.1, bf16[64,4096]{1,0:T(8,128)(2,1)} %refs_3_.1, ...), custom_call_target="tpu_custom_call" | custom-call | tf_op jit(solution)/shard_map/pallas_call | solution.py:464
  88.4 2.1 %shard_map.174 = (bf16[128,4096]{1,0:T(8,128)(2,1)}, bf16[128,512]{1,0:T(8,128)(2,1)}, bf16[128,512]{1,0:T(8,128)(2,1)}, f32[1,128]{1,0:T(1,128)}, f32[1,128]{1,0:T(1,128)}) custom-call(bf16[128,4096]{1,0:T(8,128)(2,1)} %get-tuple-element.15.refs_0_, bf16[128,512]{1,0:T(8,128)(2,1)} %get-tuple-element.16.refs_1_, ...), custom_call_target="tpu_custom_call" | custom-call | tf_op jit(solution)/shard_map/pallas_call | solution.py:545

commit v6 on v5

--- a/solution.py
+++ b/solution.py
@@ -303,8 +303,8 @@
 
     @pl.loop(0, 4)
     def _(step):
-        c = lax.rem(lax.div(me, 8) + 6 + lax.div(step + 1, 2) * (1 - 2 * lax.rem(step, 2)), 4)
-
+        turn = (1 - 2 * lax.rem(step, 2)) * (1 - 2 * lax.rem(lax.div(me, NY), 2))
+        c = lax.rem(lax.div(me, 8) + 6 + lax.div(step + 1, 2) * turn, 4)
         mine = c == lax.div(me, 8)
 
         @pl.when(mine)

time: 91.1 us -> 90.4 us (level)
  no operation moved by 1% of the time
where the time goes in v6:
time: 90.4 us; the launch traced here: 90.3 us
  Pallas kernels  89.6 us (99%)
    pallas_call x1, Pallas kernels, body(): pl.pallas_call(kernel, out_shape=(jax.ShapeDtypeStruct((128, 4096), BF),...  87.5 us
    pallas_call x1, Pallas kernels, body(): pl.pallas_call(write_out, out_shape=tuple((jax.ShapeDtypeStruct(x.shape,...  2.14 us

profile of v6, /device:TPU:1, one launch (start us, length us, event | category | flops | bytes accessed | tf_op | source)
XLA Modules:
  0.0 90.3 jit_solution(3231227623307363274)
XLA Ops:
  0.6 87.5 %shard_map.173 = (bf16[128,4096]{1,0:T(8,128)(2,1)}, bf16[128,512]{1,0:T(8,128)(2,1)}, bf16[128,512]{1,0:T(8,128)(2,1)}, f32[1,128]{1,0:T(1,128)}, f32[1,128]{1,0:T(1,128)}) custom-call(bf16[64,4096]{1,0:T(8,128)(2,1)} %refs_0_.1, bf16[64,512]{1,0:T(8,128)(2,1)} %refs_1_.1, bf16[64,512]{1,0:T(8,128)(2,1)} %refs_2_.1, bf16[64,4096]{1,0:T(8,128)(2,1)} %refs_3_.1, ...), custom_call_target="tpu_custom_call" | custom-call | tf_op jit(solution)/shard_map/pallas_call | solution.py:464
  88.1 2.1 %shard_map.174 = (bf16[128,4096]{1,0:T(8,128)(2,1)}, bf16[128,512]{1,0:T(8,128)(2,1)}, bf16[128,512]{1,0:T(8,128)(2,1)}, f32[1,128]{1,0:T(1,128)}, f32[1,128]{1,0:T(1,128)}) custom-call(bf16[128,4096]{1,0:T(8,128)(2,1)} %get-tuple-element.15.refs_0_, bf16[128,512]{1,0:T(8,128)(2,1)} %get-tuple-element.16.refs_1_, ...), custom_call_target="tpu_custom_call" | custom-call | tf_op jit(solution)/shard_map/pallas_call | solution.py:545

commit v7 on v6

--- a/solution.py
+++ b/solution.py
@@ -35,9 +35,11 @@
     return r * scaled - x * (r * r * r) * inner
 
 
-def attend_keys(q, cot, gain, keys, vals, mask):
+def attend_keys(q, cot, gain, keys, vals, causal, last):
     qn = (q * inverse_norm(q) * gain).astype(BF)
-    weights = jnp.exp(contract(keys, qn, 1, 1) * SCALE) * mask
+    raw = jnp.exp(contract(keys, qn, 1, 1) * SCALE)
+    middle = [raw[64:128]] if keys.shape[0] == 192 else []
+    weights = jnp.concatenate([raw[:64] * causal, *middle, raw[-64:] * last], axis=0)
     probs = weights * (1.0 / jnp.sum(weights, axis=0, keepdims=True))
     dprob = contract(vals, cot, 1, 1)
     inner = jnp.sum(probs * dprob, axis=0, keepdims=True)
@@ -273,8 +275,7 @@
         far_k = above_rows(0, 0, c)
         keys = jnp.concatenate([own_k, far_k], axis=0)
         vals = jnp.concatenate([pkv[1, :, col(c, 0)], above_rows(0, 1, c)], axis=0)
-        mask = jnp.concatenate([causal[...], jnp.full((64, 512), 1.0, F32) * above], axis=0)
-        dscore, dk, dv = attend_keys(q, cot, qgain, keys, vals, mask)
+        dscore, dk, dv = attend_keys(q, cot, qgain, keys, vals, causal[...], above)
         dq = attend_queries(q, qgain, keys, dscore)
         for h in range(8):
             out_q[0:64, col(8 * c, h)] = dq[h * 64:(h + 1) * 64].astype(BF)
@@ -326,9 +327,7 @@
         vals = jnp.concatenate(
             [contract(back, own_rows(8 * c + 4), 1, 0).astype(BF), above_rows(1, 1, c), above_rows(2, 1, c)], axis=0
         )
-        ones = jnp.full((64, 512), 1.0, F32)
-        mask = jnp.concatenate([causal[...], ones, ones * upper_ok], axis=0)
-        dscore, dk, dv = attend_keys(q, cot, qgain, keys, vals, mask)
+        dscore, dk, dv = attend_keys(q, cot, qgain, keys, vals, causal[...], upper_ok)
         for b in range(4):
             for j in range(2):
                 at = 64 + 64 * j + 16 * b
@@ -404,20 +403,24 @@
 
     rd[group] = gd[...]
 
-    await_all(recv.at[7], others(r4))
+    xs = [pre_k[:, c * 128:(c + 1) * 128].astype(F32) for c in range(4)]
+    rs = [inverse_norm(x) for x in xs]
+    await_all(send.at[5], near_others(rt12))
+    await_all(send.at[6], others(rg))
+
     def far_rows(which, c):
         pairs = [r4[4 * b + c, which].astype(F32) + r4[NEAR + 4 * b + c, which].astype(F32) for b in range(4)]
         return jnp.concatenate(pairs, axis=0)
 
+    await_all(recv.at[7], others(r4))
     for c in range(4):
         cols = slice(c * 128, (c + 1) * 128)
-        x = pre_k[:, cols].astype(F32)
-        dk = dkp[:, cols] + far_rows(0, c)
-        out_k[0:64, cols] = norm_back(x, inverse_norm(x), kgain, dk).astype(BF)
         out_v[0:64, cols] = (dvp[:, cols] + far_rows(1, c)).astype(BF)
-
+    stores[4].start()
+    for c in range(4):
+        cols = slice(c * 128, (c + 1) * 128)
+        out_k[0:64, cols] = norm_back(xs[c], rs[c], kgain, dkp[:, cols] + far_rows(0, c)).astype(BF)
     stores[3].start()
-    stores[4].start()
 
     await_all(dsem.at[1], rd.at[pl.ds(0, n_dp - 1)])
 
@@ -427,8 +430,6 @@
     stores[5].start()
     stores[6].start()
 
-    await_all(send.at[5], near_others(rt12))
-    await_all(send.at[6], others(rg))
     await_all(send.at[7], others(r4))
     await_all(dsem.at[0], rd.at[pl.ds(0, n_dp - 1)])
     for each in stores:

time: 90.4 us -> 90.4 us (level)
  no operation moved by 1% of the time
where the time goes in v7:
time: 90.4 us; the launch traced here: 90.3 us
  Pallas kernels  89.6 us (99%)
    pallas_call x1, Pallas kernels, body(): pl.pallas_call(kernel, out_shape=(jax.ShapeDtypeStruct((128, 4096), BF),...  87.5 us
    pallas_call x1, Pallas kernels, body(): pl.pallas_call(write_out, out_shape=tuple((jax.ShapeDtypeStruct(x.shape,...  2.14 us

profile of v7, /device:TPU:1, one launch (start us, length us, event | category | flops | bytes accessed | tf_op | source)
XLA Modules:
  0.0 90.3 jit_solution(10926658239463025176)
XLA Ops:
  0.6 87.5 %shard_map.173 = (bf16[128,4096]{1,0:T(8,128)(2,1)}, bf16[128,512]{1,0:T(8,128)(2,1)}, bf16[128,512]{1,0:T(8,128)(2,1)}, f32[1,128]{1,0:T(1,128)}, f32[1,128]{1,0:T(1,128)}) custom-call(bf16[64,4096]{1,0:T(8,128)(2,1)} %refs_0_.1, bf16[64,512]{1,0:T(8,128)(2,1)} %refs_1_.1, bf16[64,512]{1,0:T(8,128)(2,1)} %refs_2_.1, bf16[64,4096]{1,0:T(8,128)(2,1)} %refs_3_.1, ...), custom_call_target="tpu_custom_call" | custom-call | tf_op jit(solution)/shard_map/pallas_call | solution.py:465
  88.1 2.1 %shard_map.174 = (bf16[128,4096]{1,0:T(8,128)(2,1)}, bf16[128,512]{1,0:T(8,128)(2,1)}, bf16[128,512]{1,0:T(8,128)(2,1)}, f32[1,128]{1,0:T(1,128)}, f32[1,128]{1,0:T(1,128)}) custom-call(bf16[128,4096]{1,0:T(8,128)(2,1)} %get-tuple-element.15.refs_0_, bf16[128,512]{1,0:T(8,128)(2,1)} %get-tuple-element.16.refs_1_, ...), custom_call_target="tpu_custom_call" | custom-call | tf_op jit(solution)/shard_map/pallas_call | solution.py:546
